TPU v7x, 512 devices: a whole 4x8x8 slice. The times are simulated.
512 devices in a mesh: grp: 8 (over y), sub: 64 (over z, x, core).
Axes of the slice: x: 4, y: 8, z: 8, core: 2. Of those that a mesh axis runs over, the one named last changes fastest.
Arguments:
- coupling: bfloat16 [16384, 192, 192], P(('grp', 'sub')), may hold values from -0.4375 to 0.4375
- factors: bfloat16 [2048, 192, 192], P(('grp', 'sub'))
- face_diag: float32 [16384, 192], P(('grp', 'sub')), may hold values from 4 to 16
- face_block: int32 [16384], P(('grp', 'sub')), may hold values from 0 to 3
- face_owner: int32 [16384, 1], P(('grp', 'sub')), may hold values from 0 to 63; in each aligned block of 32 rows (0 to 31, 32 to 63, ...) at most 2 rows name the same one
- owner_slot: int32 [16384], P(('grp', 'sub')), may hold values from 0 to 11
- coarse_basis: bfloat16 [6144, 192, 128], P(('grp', 'sub')), may hold values from -0.03125 to 0.03125
- coarse_index: int32 [65536], P(('grp', 'sub')), may hold values from 0 to 767, as said below
- projection: bfloat16 [6144, 256], P('grp'), may hold values from -1 to 1
Outputs:
- owned_schur: bfloat16 [6144, 192, 192], P(('grp', 'sub'))
- top_coarse: float32 [256, 256], replicated
Inputs may be any that keep to these rules, and one draw needn't show every extreme that they name: `face_owner`: among the faces of one subdomain no owner is named more than 2 times, and some subdomain names some owner exactly 2 times. `coarse_index`: the 128 entries of one subdomain are distinct.
All inputs are finite; a program needn't handle non-finite values.
Results may differ from a plain program's by a relative error of at most 0.0034.
Values may be sent and summed in bfloat16 or wider, within the bound.
No kernel may reach another device: no remote copies, remote signals or barrier semaphores. Data moves between devices by JAX's collectives and lax.ppermute only.
A program may use at most 128 MiB of HBM per device.

v0:
```python
import jax
import jax.numpy as jnp
from jax import lax
from jax.sharding import PartitionSpec as P

CAP = 2


def place_rows(values, position, slot_total):
    empty = jnp.zeros((slot_total,) + values.shape[1:], values.dtype)
    return empty.at[position].set(values)


def local(
    coupling,
    factors,
    face_diag,
    face_block,
    face_owner,
    owner_slot,
    coarse_basis,
    coarse_index,
    projection,
):
    peer_count = lax.axis_size("sub")
    face_count, face_width = face_diag.shape
    owned_count = coarse_basis.shape[0]
    slot_total = peer_count * CAP
    picked = factors[face_block]
    interior = jnp.einsum(
        "fij,fjk->fik", picked, coupling, preferred_element_type=jnp.float32
    ).astype(jnp.bfloat16)
    correction = jnp.einsum("fij,fik->fjk", interior, interior, preferred_element_type=jnp.float32)
    identity = jnp.eye(face_width, dtype=jnp.float32)
    schur = (face_diag[:, :, None] * identity - correction).astype(jnp.bfloat16)
    owner_ids = face_owner[:, 0]
    member = (owner_ids[:, None] == lax.iota(jnp.int32, peer_count)[None, :]).astype(jnp.int32)
    before = jnp.cumsum(member, axis=0) - member
    position = owner_ids * CAP + jnp.sum(before * member, axis=1)
    slot_empty = jnp.full((slot_total,), -1.0, jnp.bfloat16)
    slot_send = (
        slot_empty.at[position].set(owner_slot.astype(jnp.bfloat16)).reshape(peer_count, CAP)
    )
    send_full = place_rows(schur, position, slot_total).reshape(
        peer_count, CAP, face_width, face_width
    )
    got_full, got_slots = (
        lax.all_to_all(send_full, "sub", split_axis=0, concat_axis=0, tiled=True),
        lax.all_to_all(slot_send, "sub", split_axis=0, concat_axis=0, tiled=True),
    )
    arrived = got_full.reshape(slot_total, face_width, face_width)
    slot_labels = lax.iota(jnp.float32, owned_count).astype(jnp.bfloat16)
    select = (got_slots.reshape(1, slot_total) == slot_labels[:, None]).astype(jnp.bfloat16)
    summed = jnp.dot(
        select,
        arrived.reshape(slot_total, face_width * face_width),
        preferred_element_type=jnp.float32,
    )
    assembled = summed.reshape(owned_count, face_width, face_width).astype(jnp.bfloat16)
    applied = jnp.einsum(
        "sij,sjc->sic", assembled, coarse_basis, preferred_element_type=jnp.float32
    ).astype(jnp.bfloat16)
    local_coarse = jnp.einsum(
        "sic,sie->ce", coarse_basis, applied, preferred_element_type=jnp.float32
    )
    group_size = projection.shape[0]
    placement = (coarse_index[:, None] == lax.iota(jnp.int32, group_size)[None, :]).astype(
        jnp.float32
    )
    proj_f = projection.astype(jnp.float32)
    basis_rows = jnp.dot(placement, proj_f, precision=lax.Precision.HIGHEST)
    inner_side = jnp.dot(local_coarse, basis_rows, precision=lax.Precision.HIGHEST)
    own_top = jnp.dot(basis_rows.T, inner_side, precision=lax.Precision.HIGHEST)
    top_matrix = lax.psum(own_top, ("grp", "sub"))
    return (assembled, top_matrix)


def solution(mesh):
    return jax.shard_map(
        local,
        mesh=mesh,
        in_specs=(
            P(("grp", "sub"), None, None),
            P(("grp", "sub"), None, None),
            P(("grp", "sub"), None),
            P(("grp", "sub")),
            P(("grp", "sub"), None),
            P(("grp", "sub")),
            P(("grp", "sub"), None, None),
            P(("grp", "sub")),
            P("grp", None),
        ),
        out_specs=(P(("grp", "sub"), None, None), P()),
        check_vma=False,
    )
```

profile of v0, /device:TPU:1, one launch (start us, length us, event | category | flops | bytes accessed | tf_op | source)
XLA Modules:
  0.0 663.9 jit_solution(13051048870271773794)
XLA Ops:
  7.2 0.0 copy-start
  7.2 0.9 fusion.11
  8.1 0.1 reduce_window_sum.11
  8.1 0.9 select_reduce_fusion
  9.0 0.7 fusion.16
  9.6 0.7 convert_element_type.36
  10.3 0.8 scatter_custom_fusion
  11.1 0.8 all_to_all.12
  11.8 14.8 %all-to-all-start = ((bf16[64,1,2]{2,1,0:T(2,128)(2,1)}), bf16[64,1,2]{2,1,0:T(2,128)(2,1)S(1)}, u32[]{:S(2)}, u32[]{:S(2)}) async-start(bf16[64,1,2]{2,1,0:T(2,128)(2,1)} %all_to_all.12), calls=%async_computation | async-start | bytes 65536 | tf_op jit(solution)/shard_map/all_to_all | solution.py:49
  26.7 0.7 compare_select_fusion
  27.4 0.0 copy-start.2
  27.4 3.5 gather_fusion
  30.8 0.0 copy-done
  30.8 0.0 copy-done.2
  30.8 7.4 %subtract_convert_fusion = bf16[32,192,192]{2,1,0:T(8,128)(2,1)} fusion(f32[192,192]{1,0:T(8,128)S(1)} %fusion.10, f32[32,192]{1,0:T(8,128)S(1)} %copy-done.2, bf16[32,192,192]{2,1,0:T(8,128)(2,1)} %gather_fusion, bf16[32,192,192]{2,1,0:T(8,128)(2,1)S(1)} %copy-done), kind=kOutput, calls=%fused_computation.3 | convolution fusion | flops 910688256 | bytes 7249920 | tf_op jit(solution)/shard_map/fij,fik->fjk/dot_general | solution.py:33
  38.3 6.0 broadcast_in_dim.7
  44.3 10.3 %scatter_fusion = bf16[128,192,192]{2,1,0:T(8,128)(2,1)} fusion(bf16[128,192,192]{2,1,0:T(8,128)(2,1)} %broadcast_in_dim.7, s32[32]{0:T(128)S(1)} %fusion.16, bf16[32,192,192]{2,1,0:T(8,128)(2,1)} %subtract_convert_fusion), kind=kCustom, calls=%fused_computation.2 | custom fusion | bytes 7078016 | tf_op jit(solution)/shard_map/scatter | solution.py:11
  54.6 0.0 all-to-all-done
  54.6 0.0 copy-start.1
  54.6 10.6 %all-to-all-start.1 = ((bf16[64,2,192,192]{3,2,1,0:T(8,128)(2,1)}), bf16[64,2,192,192]{3,2,1,0:T(8,128)(2,1)}, u32[]{:S(2)}, u32[]{:S(2)}) async-start(bf16[64,2,192,192]{3,2,1,0:T(8,128)(2,1)} %bitcast.28), calls=%async_computation.1 | async-start | bytes 25165824 | tf_op jit(solution)/shard_map/all_to_all | solution.py:48
  65.2 0.0 all-reduce.2.cloned.1.call-start
  65.3 0.0 copy-done.1
  65.3 1.2 fusion.8
  66.6 0.1 reduce
  66.7 0.1 eq.54
  66.8 272.9 %all-to-all-done.1 = bf16[64,2,192,192]{3,2,1,0:T(8,128)(2,1)} async-done(((bf16[64,2,192,192]{3,2,1,0:T(8,128)(2,1)}), bf16[64,2,192,192]{3,2,1,0:T(8,128)(2,1)}, u32[]{:S(2)}, u32[]{:S(2)}) %all-to-all-start.1) | async-done | bytes 9437216 | tf_op jit(solution)/shard_map/all_to_all | solution.py:48
  339.7 20.3 %reshape_reshape.3 = bf16[128,36864]{1,0:T(8,128)(2,1)} reshape(bf16[64,2,192,192]{3,2,1,0:T(8,128)(2,1)} %all-to-all-done.1) | data formatting | bytes 18874368 | tf_op jit(solution)/shard_map/reshape;reshape | solution.py:56
  360.0 12.7 %copy.18 = bf16[36864,128]{1,0:T(8,128)(2,1)} copy(bf16[36864,128]{0,1:T(8,128)(2,1)} %bitcast.30) | data formatting | bytes 18874368 | tf_op jit(solution)/shard_map/dot_general | solution.py:54
  372.7 8.7 %convolution_convert_fusion = bf16[12,192,192]{2,0,1:T(8,128)(2,1)S(1)} fusion(bf16[192,192,128]{2,1,0:T(8,128)(2,1)} %bitcast.29, bf16[128]{0:T(256)(128)(2,1)S(1)} %eq.54, bf16[12]{0:T(256)(128)(2,1)S(1)} %iota_convert_fusion), kind=kOutput, calls=%fused_computation.7 | convolution fusion | flops 113693184 | bytes 10322200 | tf_op jit(solution)/shard_map/dot_general | solution.py:54
  381.3 1.5 copy.20
  382.8 2.2 fusion.7
  385.0 0.3 fusion.19
  385.3 1.1 fusion.20
  386.5 0.0 all-reduce.2.cloned.1.call-update
  386.5 268.9 %all-reduce.2.cloned.1.call-done = f32[256,256]{1,0:T(8,128)} async-done(((f32[256,256]{1,0:T(8,128)}), f32[256,256]{1,0:T(8,128)}) %all-reduce.2.cloned.1.call-update) | async-done | bytes 262160 | tf_op jit(solution)/shard_map/psum | solution.py:74
  655.3 1.7 copy.24
  (3 shorter events, 0.0 us)
Async XLA Ops:
  7.2 23.7 %copy-start = (bf16[32,192,192]{2,1,0:T(8,128)(2,1)S(1)}, bf16[32,192,192]{2,1,0:T(8,128)(2,1)}, u32[]{:S(2)}) copy-start(bf16[32,192,192]{2,1,0:T(8,128)(2,1)} %param.9) | copy-start | bytes 7077892
  11.8 42.8 %all-to-all-start = ((bf16[64,1,2]{2,1,0:T(2,128)(2,1)}), bf16[64,1,2]{2,1,0:T(2,128)(2,1)S(1)}, u32[]{:S(2)}, u32[]{:S(2)}) async-start(bf16[64,1,2]{2,1,0:T(2,128)(2,1)} %all_to_all.12), calls=%async_computation | async-start | bytes 65536 | tf_op jit(solution)/shard_map/all_to_all | solution.py:49
  27.4 3.5 copy-start.2
  54.6 10.6 %copy-start.1 = (s32[128]{0:T(128)S(1)}, s32[128]{0:T(128)}, u32[]{:S(2)}) copy-start(s32[128]{0:T(128)} %param.16) | copy-start | bytes 1540
  54.6 285.1 %all-to-all-start.1 = ((bf16[64,2,192,192]{3,2,1,0:T(8,128)(2,1)}), bf16[64,2,192,192]{3,2,1,0:T(8,128)(2,1)}, u32[]{:S(2)}, u32[]{:S(2)}) async-start(bf16[64,2,192,192]{3,2,1,0:T(8,128)(2,1)} %bitcast.28), calls=%async_computation.1 | async-start | bytes 25165824 | tf_op jit(solution)/shard_map/all_to_all | solution.py:48
  65.2 590.1 %all-reduce.2.cloned.1.call-start = ((), (), s32[]{:S(2)}) async-start(), calls=%async_computation.2 | async-start | bytes 524288 | tf_op jit(solution)/shard_map/psum | solution.py:74
Sparse Core Ops, SparseCore 0:
  386.6 268.6 all-reduce.1
where the time goes:
time: 665 us; the launch traced here: 664 us
  waiting for transfers between devices  542 us (82%)
  local copies, waits for them, and re-layouts  57.6 us (9%)
  starting transfers between devices  25.4 us (4%)
  matrix products  21 us (3%)
  between operations  14.1 us (2%)
    all_to_all x1, waiting for transfers between devices, local(): lax.all_to_all(send_full, 'sub', split_axis=0, concat_axis=0, tiled=True)  273 us
    psum x1, waiting for transfers between devices, local(): top_matrix = lax.psum(own_top, ('grp', 'sub'))  269 us
    another operation x1, local copies, waits for them, and re-layouts, local(): arrived.reshape(slot_total, face_width * face_width)  20.3 us
    all_to_all x1, starting transfers between devices, local(): lax.all_to_all(slot_send, 'sub', split_axis=0, concat_axis=0, tiled=True)  14.8 us
  transfers between devices with their start and end apart: 3, of which 2 were waited for; matrix products, arithmetic and copies ran while one was open for 4% of the time, Pallas kernels for 0%

commit v1 on v0

v1 whole, which is shorter than its diff:
```python
import jax
import jax.numpy as jnp
from jax import lax
from jax.experimental import pallas as pl
from jax.experimental.pallas import tpu as pltpu
from jax.sharding import PartitionSpec as P

Q = 64
LANES = 128
STEP_FACES = 8
KEEP, OWNER_AT, SLOT_AT = 63, 61, 60
VMEM_LIMIT = 56 * 1024 * 1024
f32, bf16, i32 = jnp.float32, jnp.bfloat16, jnp.int32


def masks():
    row = lax.broadcasted_iota(i32, (Q, LANES), 0)
    lane = lax.broadcasted_iota(i32, (Q, LANES), 1)
    d = ((lane & (Q - 1)) - row) & (Q - 1)
    keep = (d < Q // 2) | ((d == Q // 2) & (row < Q // 2))
    return lane < Q, d, keep


def swap_halves(x):
    return pltpu.roll(x, Q, 1)


def schur_kernel(block_ref, owner_ref, slot_ref, coupling_ref, factors_ref, diag_ref, out_ref, scratch):
    step = pl.program_id(0)
    left, d, keep = masks()
    eye = d == 0
    pairs = out_ref.shape[1] // 5
    for pair in range(STEP_FACES // 2):
        last = None
        for odd in range(2):
            q = pair * 2 + odd
            face = step * STEP_FACES + q
            c = coupling_ref[q]
            mid = c[:, Q : 2 * Q]
            columns = jnp.concatenate([c[:, 2 * Q :], mid, mid, c[:, :Q]], axis=1)
            interior = jnp.dot(
                factors_ref[block_ref[face]], columns, preferred_element_type=f32
            ).astype(bf16)
            g = lax.dot_general(
                interior, interior, (((0,), (0,)), ((), ())), preferred_element_type=f32
            )
            d3, r1 = g[:Q, :LANES], g[Q : 2 * Q, :LANES]
            t0, d1 = g[3 * Q :, :LANES], g[3 * Q :, LANES:]
            diag01 = diag_ref[q : q + 1, :LANES]
            diag2 = jnp.concatenate([diag_ref[q : q + 1, LANES:]] * 2, axis=1)
            t1 = jnp.where(eye & ~left, swap_halves(diag01), 0.0) - jnp.where(
                left | ~keep, r1, d1
            )
            d2_diag = jnp.sum(
                jnp.where(eye & ~left, diag01 - r1, 0.0), axis=1, keepdims=True
            )
            spare = jnp.where(
                d == KEEP,
                d2_diag,
                jnp.where(
                    d == OWNER_AT,
                    owner_ref[face].astype(f32),
                    jnp.where(d == SLOT_AT, slot_ref[face].astype(f32), 0.0),
                ),
            )
            f = jnp.where(keep, jnp.where(eye, diag2, 0.0) - d3, spare)
            at = step * (STEP_FACES // 2) + pair

            def put(k, value):
                scratch[pl.ds(k * Q * pairs + at, Q, stride=pairs), :] = value

            put(2 * odd, -t0)
            put(2 * odd + 1, t1)
            if odd:
                put(4, jnp.where(left, last, swap_halves(f)))
            last = f

    @pl.when(step == pl.num_programs(0) - 1)
    def _():
        for k in range(5):
            out_ref[:, pairs * k : pairs * (k + 1), :] = (
                scratch[Q * pairs * k : Q * pairs * (k + 1), :]
                .reshape(Q, pairs, LANES)
                .astype(bf16)
            )


def pack_faces(face_block, owner, slot, coupling, factors, face_diag):
    faces, width, _ = coupling.shape
    blocks = factors.shape[0]
    pairs = faces // 2
    return pl.pallas_call(
        schur_kernel,
        grid_spec=pltpu.PrefetchScalarGridSpec(
            num_scalar_prefetch=3,
            grid=(faces // STEP_FACES,),
            in_specs=[
                pl.BlockSpec((STEP_FACES, width, width), lambda s, *_: (s, 0, 0)),
                pl.BlockSpec((blocks, width, width), lambda s, *_: (0, 0, 0)),
                pl.BlockSpec((STEP_FACES, width), lambda s, *_: (s, 0)),
            ],
            out_specs=pl.BlockSpec((Q, 5 * pairs, LANES), lambda s, *_: (0, 0, 0)),
            scratch_shapes=[pltpu.VMEM((5 * Q * pairs, LANES), f32)],
        ),
        out_shape=jax.ShapeDtypeStruct((Q, 5 * pairs, LANES), bf16),
        compiler_params=pltpu.CompilerParams(vmem_limit_bytes=VMEM_LIMIT),
        name="pack_faces",
    )(face_block, owner, slot, coupling, factors, face_diag)


def merge_kernel(me_ref, x_ref, out_ref, flat):
    peers, rows, _ = x_ref.shape
    pairs = rows // 5
    total = peers * pairs
    slots = 12
    me = me_ref[0]

    def piece(k):
        return x_ref[:, pairs * k : pairs * (k + 1), :].reshape(total, LANES)

    shared = piece(4)
    which = lax.broadcasted_iota(i32, (8, LANES), 0)
    lane = lax.broadcasted_iota(i32, (8, LANES), 1)
    place = ((me + jnp.where((which & 1) == 0, OWNER_AT, SLOT_AT)) & (Q - 1)) + jnp.where(
        which < 2, 0, Q
    )
    pick = ((lane == place) & (which < 4)).astype(f32).astype(bf16)
    named = lax.dot_general(
        pick, shared, (((1,), (1,)), ((), ())), preferred_element_type=f32
    ).astype(i32)
    target = lax.broadcasted_iota(i32, (slots * peers, total), 0)
    even = (target == named[1:2] * peers + named[0:1]).astype(f32).astype(bf16)
    odd = (target == named[3:4] * peers + named[2:3]).astype(f32).astype(bf16)
    sums = []
    for k in range(2):
        sums.append(
            jnp.dot(even, piece(k), preferred_element_type=f32)
            + jnp.dot(odd, piece(2 + k), preferred_element_type=f32)
        )
    low = jnp.dot(even, shared, preferred_element_type=f32)
    high = jnp.dot(odd, shared, preferred_element_type=f32)
    half = slots // 2
    first = half * peers
    left = lax.broadcasted_iota(i32, (first, LANES), 1) < Q
    sums.append(
        jnp.where(
            left,
            low[:first] + swap_halves(high[:first]),
            swap_halves(low[first:]) + high[first:],
        )
    )
    out_rows = out_ref.shape[1]
    for k in range(3):
        for s in range(sums[k].shape[0] // peers):
            flat[pl.ds(slots * k + s, peers, stride=out_rows), :] = sums[k][
                peers * s : peers * (s + 1), :
            ]
    for s in range(slots * 2 + half, out_rows):
        flat[pl.ds(s, peers, stride=out_rows), :] = jnp.zeros((peers, LANES), f32)
    out_ref[...] = flat[...].reshape(peers, out_rows, LANES).astype(bf16)


def merge_rows(me, x):
    peers = x.shape[0]
    return pl.pallas_call(
        merge_kernel,
        in_specs=[
            pl.BlockSpec(memory_space=pltpu.SMEM),
            pl.BlockSpec(memory_space=pltpu.VMEM),
        ],
        out_specs=pl.BlockSpec(memory_space=pltpu.VMEM),
        scratch_shapes=[pltpu.VMEM((peers * 32, LANES), f32)],
        out_shape=jax.ShapeDtypeStruct((peers, 32, LANES), bf16),
        compiler_params=pltpu.CompilerParams(vmem_limit_bytes=VMEM_LIMIT),
        name="merge_rows",
    )(me, x)


def split3(x):
    a = x.astype(bf16)
    rest = x - a.astype(f32)
    b = rest.astype(bf16)
    return a, b, (rest - b.astype(f32)).astype(bf16)


def coarse_kernel(z_ref, basis_ref, rows_ref, owned_ref, top_ref, flat, applied):
    slots, width, coarse = basis_ref.shape
    half = slots // 2
    step = z_ref.shape[1]
    left, d, keep = masks()
    eye = d == 0
    flat[...] = z_ref[...].reshape(Q * step, LANES).astype(f32)
    for q in range(half):
        f_both = flat[pl.ds(slots * 2 + q, Q, stride=step), :]
        f_turned = f_both.T
        for r in (q, q + half):
            t0 = flat[pl.ds(r, Q, stride=step), :]
            t1 = flat[pl.ds(slots + r, Q, stride=step), :]
            turned = jnp.concatenate([t0, t1], axis=0).T
            lower = turned[Q:]
            if r == q:
                f, f_t = f_both, f_turned[:Q]
            else:
                f, f_t = swap_halves(f_both), f_turned[Q:]
            d2_diag = jnp.sum(
                jnp.where((d == KEEP) & left, f, 0.0), axis=1, keepdims=True
            )
            d1 = swap_halves(jnp.where(keep, t1, lower))
            d2 = jnp.where(eye, d2_diag, jnp.where(keep, lower, t1))
            d3 = jnp.where(keep[:, :Q], f[:, :Q], f_t)
            owned_ref[r, :Q, :LANES] = jnp.where(left, d1, t0).astype(bf16)
            owned_ref[r, :Q, LANES:] = t0[:, :Q].astype(bf16)
            owned_ref[r, Q : 2 * Q, :LANES] = jnp.where(left, lower, d2).astype(bf16)
            owned_ref[r, Q : 2 * Q, LANES:] = t1[:, :Q].astype(bf16)
            owned_ref[r, 2 * Q :, :LANES] = turned[:Q].astype(bf16)
            owned_ref[r, 2 * Q :, LANES:] = d3.astype(bf16)
    for r in range(slots):
        applied[r] = jnp.dot(
            owned_ref[r], basis_ref[r], preferred_element_type=f32
        ).astype(bf16)
    local_coarse = lax.dot_general(
        basis_ref[...].reshape(slots * width, coarse),
        applied[...].reshape(slots * width, coarse),
        (((0,), (0,)), ((), ())),
        preferred_element_type=f32,
    )
    rows_t = rows_ref[...]
    inner = 0.0
    for part in split3(local_coarse):
        inner += lax.dot_general(
            part, rows_t, (((1,), (1,)), ((), ())), preferred_element_type=f32
        )
    top = 0.0
    for part in split3(inner):
        top += jnp.dot(rows_t, part, preferred_element_type=f32)
    size = top.shape[0]
    for k in range(size // LANES):
        top_ref[size * k : size * (k + 1), :] = top[:, LANES * k : LANES * (k + 1)]


def owned_and_top(z, basis, rows_t):
    slots, width, coarse = basis.shape
    size = rows_t.shape[0]
    vmem = pl.BlockSpec(memory_space=pltpu.VMEM)
    return pl.pallas_call(
        coarse_kernel,
        in_specs=[vmem, vmem, vmem],
        out_specs=[vmem, vmem],
        scratch_shapes=[
            pltpu.VMEM((Q * z.shape[1], LANES), f32),
            pltpu.VMEM((slots, width, coarse), bf16),
        ],
        out_shape=[
            jax.ShapeDtypeStruct((slots, width, width), bf16),
            jax.ShapeDtypeStruct((size * size // LANES, LANES), f32),
        ],
        compiler_params=pltpu.CompilerParams(vmem_limit_bytes=VMEM_LIMIT),
        name="owned_and_top",
    )(z, basis, rows_t)


def exchange(x, axis):
    return lax.all_to_all(x, axis, split_axis=0, concat_axis=0, tiled=True)


def local(
    coupling,
    factors,
    face_diag,
    face_block,
    face_owner,
    owner_slot,
    coarse_basis,
    coarse_index,
    projection,
):
    peers, groups = lax.axis_size("sub"), lax.axis_size("grp")
    me = lax.axis_index("sub").astype(i32).reshape(1)
    x = pack_faces(face_block, face_owner[:, 0], owner_slot, coupling, factors, face_diag)
    x = exchange(x, "sub")
    group_size, size = projection.shape
    placement = (coarse_index[:, None] == lax.iota(i32, group_size)[None, :]).astype(bf16)
    rows_t = lax.dot_general(
        projection, placement, (((0,), (1,)), ((), ())), preferred_element_type=f32
    ).astype(bf16)
    z = exchange(merge_rows(me, x), "sub")
    owned, top = owned_and_top(z, coarse_basis, rows_t)
    share = size * size // LANES // peers
    part = jnp.sum(exchange(top.reshape(peers, share, LANES), "sub"), axis=0)
    part = jnp.sum(
        exchange(jnp.broadcast_to(part, (groups, share, LANES)), "grp"), axis=0
    )
    full = exchange(jnp.broadcast_to(part, (peers, share, LANES)), "sub")
    full = full.reshape(size // LANES, size, LANES)
    top_matrix = jnp.concatenate([full[k] for k in range(size // LANES)], axis=1)
    return owned, top_matrix


def solution(mesh):
    return jax.shard_map(
        local,
        mesh=mesh,
        in_specs=(
            P(("grp", "sub"), None, None),
            P(("grp", "sub"), None, None),
            P(("grp", "sub"), None),
            P(("grp", "sub")),
            P(("grp", "sub"), None),
            P(("grp", "sub")),
            P(("grp", "sub"), None, None),
            P(("grp", "sub")),
            P("grp", None),
        ),
        out_specs=(P(("grp", "sub"), None, None), P()),
        check_vma=False,
    )
```

time: 665 us -> 147 us (0.22)
  waiting for transfers between devices: 542 us -> 50.3 us
  local copies, waits for them, and re-layouts: 57.6 us -> 1.93 us
  blocking collectives: 0 us -> 51.5 us
  matrix products: 21 us -> 0.99 us
  Pallas kernels: 0 us -> 19.4 us
  between operations: 14.1 us -> 0.69 us
    psum x1 -> x0, waiting for transfers between devices: 269 us -> none  [local(): top_matrix = lax.psum(own_top, ('grp', 'sub'))]
    all_to_all x2, waiting for transfers between devices: 273 us -> 50.3 us  [exchange(): return lax.all_to_all(x, axis, split_axis=0, concat_axis=0, tiled=True)]
    all_to_all x0 -> x3, blocking collectives: none -> 51.5 us  [exchange(): return lax.all_to_all(x, axis, split_axis=0, concat_axis=0, tiled=True)]
    another operation x1 -> x0, local copies, waits for them, and re-layouts: 20.3 us -> none  [local(): arrived.reshape(slot_total, face_width * face_width)]
    dot_general x6 -> x1, matrix products: 21 us -> 0.99 us  [local(): lax.dot_general(projection, placement, (((0,), (1,)), ((), ())), preferre...]
    pallas_call x0 -> x3, Pallas kernels: none -> 19.4 us  [the longest x1 9.53 us: pack_faces(): pl.pallas_call(schur_kernel, grid_spec=pltpu.PrefetchScalarGridSpec(num_s...]
    dot_general x1 -> x0, local copies, waits for them, and re-layouts: 12.7 us -> none  [local(): jnp.dot(select, arrived.reshape(slot_total, face_width * face_width), pre...]
    scatter x2 -> x0, local copies, waits for them, and re-layouts: 11.1 us -> none  [the longest x1 10.3 us: place_rows(): return empty.at[position].set(values)]
  transfers between devices with their start and end apart: 3 -> 2, of which waited for: 2 -> 2; matrix products, arithmetic and copies ran while one was open for 4% -> 1% of each run, Pallas kernels for 0% -> 0%
where the time goes in v1:
time: 147 us
  blocking collectives  51.5 us (35%)
  waiting for transfers between devices  50.3 us (34%)
  starting transfers between devices  21.2 us (14%)
  Pallas kernels  19.4 us (13%)
  local copies, waits for them, and re-layouts  1.93 us (1%)
    all_to_all x3, blocking collectives, exchange(): return lax.all_to_all(x, axis, split_axis=0, concat_axis=0, tiled=True)  51.5 us
    all_to_all x2, waiting for transfers between devices, exchange(): return lax.all_to_all(x, axis, split_axis=0, concat_axis=0, tiled=True)  50.3 us
    all_to_all x2, starting transfers between devices, exchange(): return lax.all_to_all(x, axis, split_axis=0, concat_axis=0, tiled=True)  21.2 us
    pallas_call x1, Pallas kernels, pack_faces(): pl.pallas_call(schur_kernel, grid_spec=pltpu.PrefetchScalarGridSpec(num_s...  9.53 us
    pallas_call x1, Pallas kernels, merge_rows(): pl.pallas_call(merge_kernel, in_specs=[pl.BlockSpec(memory_space=pltpu.SM...  5.54 us
    pallas_call x1, Pallas kernels, owned_and_top(): pl.pallas_call(coarse_kernel, in_specs=[vmem, vmem, vmem], out_specs=[vme...  4.33 us
  transfers between devices with their start and end apart: 2, of which 2 were waited for; matrix products, arithmetic and copies ran while one was open for 1% of the time, Pallas kernels for 0%

profile of v1, /device:TPU:1, one launch (start us, length us, event | category | flops | bytes accessed | tf_op | source)
XLA Modules:
  0.0 146.8 jit_solution(16687533162239736310)
XLA Ops:
  0.6 0.0 copy-start
  0.6 9.5 %pack_faces.1 = bf16[64,80,128]{2,1,0:T(8,128)(2,1)} custom-call(s32[32]{0:T(128)} %block_ref.1, s32[32]{0:T(128)} %bitcast.11, s32[32]{0:T(128)} %slot_ref.1, bf16[32,192,192]{2,1,0:T(8,128)(2,1)} %coupling_ref.1, bf16[4,192,192]{2,1,0:T(8,128)(2,1)} %factors_ref.1, f32[32,192]{1,0:T(8,128)} %diag_ref.1), custom_call_target="tpu_custom_call" | custom-call | tf_op jit(solution)/shard_map/pack_faces/pallas_call | solution.py:92
  10.2 14.8 %all-to-all-start = ((bf16[64,80,128]{2,1,0:T(8,128)(2,1)}), bf16[64,80,128]{2,1,0:T(8,128)(2,1)S(1)}, u32[]{:S(2)}, u32[]{:S(2)}) async-start(bf16[64,80,128]{2,1,0:T(8,128)(2,1)} %pack_faces.1), calls=%async_computation | async-start | bytes 2621440 | tf_op jit(solution)/shard_map/all_to_all | solution.py:263
  25.0 33.6 %all-to-all-done.x_ref = bf16[64,80,128]{2,1,0:T(8,128)(2,1)S(1)} async-done(((bf16[64,80,128]{2,1,0:T(8,128)(2,1)}), bf16[64,80,128]{2,1,0:T(8,128)(2,1)S(1)}, u32[]{:S(2)}, u32[]{:S(2)}) %all-to-all-start) | async-done | bytes 1310752 | tf_op jit(solution)/shard_map/all_to_all | solution.py:263
  58.6 0.0 copy-start.1
  58.6 1.1 copy-done.1
  59.7 0.0 copy-start.3
  59.7 5.5 %merge_rows.1 = bf16[64,32,128]{2,1,0:T(8,128)(2,1)} custom-call(s32[1]{0:T(128)} %bitcast.me_ref, bf16[64,80,128]{2,1,0:T(8,128)(2,1)} %copy-done.1), custom_call_target="tpu_custom_call" | custom-call | tf_op jit(solution)/shard_map/merge_rows/pallas_call | solution.py:165
  65.2 6.3 %all-to-all-start.1 = ((bf16[64,32,128]{2,1,0:T(8,128)(2,1)}), bf16[64,32,128]{2,1,0:T(8,128)(2,1)S(1)}, u32[]{:S(2)}, u32[]{:S(2)}) async-start(bf16[64,32,128]{2,1,0:T(8,128)(2,1)} %merge_rows.1), calls=%async_computation.1 | async-start | bytes 1048576 | tf_op jit(solution)/shard_map/all_to_all | solution.py:263
  71.6 0.0 copy-done
  71.6 0.0 copy-done.3
  71.6 1.0 fusion.rows_ref
  72.6 16.7 %all-to-all-done.1.z_ref = bf16[64,32,128]{2,1,0:T(8,128)(2,1)S(1)} async-done(((bf16[64,32,128]{2,1,0:T(8,128)(2,1)}), bf16[64,32,128]{2,1,0:T(8,128)(2,1)S(1)}, u32[]{:S(2)}, u32[]{:S(2)}) %all-to-all-start.1) | async-done | bytes 524320 | tf_op jit(solution)/shard_map/all_to_all | solution.py:263
  89.3 0.0 copy-start.2
  89.3 0.8 copy-done.2
  90.1 4.3 %owned_and_top.1 = (bf16[12,192,192]{2,1,0:T(8,128)(2,1)}, f32[512,128]{1,0:T(8,128)}) custom-call(bf16[64,32,128]{2,1,0:T(8,128)(2,1)} %copy-done.2, bf16[12,192,128]{2,1,0:T(8,128)(2,1)} %basis_ref.1, bf16[256,128]{1,0:T(8,128)(2,1)} %fusion.rows_ref), custom_call_target="tpu_custom_call" | custom-call | tf_op jit(solution)/shard_map/owned_and_top/pallas_call | solution.py:245
  94.4 18.9 %all_to_all.25 = f32[64,8,128]{2,1,0:T(8,128)S(1)} all-to-all(f32[64,8,128]{2,1,0:T(8,128)} %bitcast.10), channel_id=1, replica_groups=mesh['grp'=8,'sub'=64] {'sub'}, dimensions={0} | all-to-all | bytes 524288 | tf_op jit(solution)/shard_map/all_to_all | solution.py:263
  113.3 0.1 reduce_sum.18
  113.4 13.5 %all_to_all.26 = f32[8,8,128]{2,1,0:T(8,128)S(1)} all-to-all(f32[8,8,128]{2,1,0:T(8,128)S(1)} %broadcast_in_dim.8), channel_id=1, replica_groups=mesh['grp'=8,'sub'=64] {'grp'}, dimensions={0} | all-to-all | bytes 65536 | tf_op jit(solution)/shard_map/all_to_all | solution.py:263
  126.9 19.1 %all_to_all.27 = f32[64,8,128]{2,1,0:T(8,128)S(1)} all-to-all(f32[64,8,128]{2,1,0:T(8,128)S(1)} %broadcast_in_dim.9), channel_id=1, replica_groups=mesh['grp'=8,'sub'=64] {'sub'}, dimensions={0} | all-to-all | bytes 524288 | tf_op jit(solution)/shard_map/all_to_all | solution.py:263
  146.0 0.7 pad_maximum_fusion
  (4 shorter events, 0.1 us)
Async XLA Ops:
  0.6 70.9 %copy-start = (bf16[768,256]{1,0:T(8,128)(2,1)S(1)}, bf16[768,256]{1,0:T(8,128)(2,1)}, u32[]{:S(2)}) copy-start(bf16[768,256]{1,0:T(8,128)(2,1)} %param.17) | copy-start | bytes 1179652
  10.2 48.4 %all-to-all-start = ((bf16[64,80,128]{2,1,0:T(8,128)(2,1)}), bf16[64,80,128]{2,1,0:T(8,128)(2,1)S(1)}, u32[]{:S(2)}, u32[]{:S(2)}) async-start(bf16[64,80,128]{2,1,0:T(8,128)(2,1)} %pack_faces.1), calls=%async_computation | async-start | bytes 2621440 | tf_op jit(solution)/shard_map/all_to_all | solution.py:263
  58.6 1.1 copy-start.1
  59.7 11.9 %copy-start.3 = (s32[128]{0:T(128)S(1)}, s32[128]{0:T(128)}, u32[]{:S(2)}) copy-start(s32[128]{0:T(128)} %param.16) | copy-start | bytes 1540
  65.2 24.0 %all-to-all-start.1 = ((bf16[64,32,128]{2,1,0:T(8,128)(2,1)}), bf16[64,32,128]{2,1,0:T(8,128)(2,1)S(1)}, u32[]{:S(2)}, u32[]{:S(2)}) async-start(bf16[64,32,128]{2,1,0:T(8,128)(2,1)} %merge_rows.1), calls=%async_computation.1 | async-start | bytes 1048576 | tf_op jit(solution)/shard_map/all_to_all | solution.py:263
  89.3 0.8 copy-start.2

commit v2 on v1

--- a/solution.py
+++ b/solution.py
@@ -7,9 +7,10 @@
 
 Q = 64
 LANES = 128
-STEP_FACES = 8
+STEP_FACES = 16
 KEEP, OWNER_AT, SLOT_AT = 63, 61, 60
-VMEM_LIMIT = 56 * 1024 * 1024
+PACK_VMEM = 56 * 1024 * 1024
+VMEM_LIMIT = 16 * 1024 * 1024
 f32, bf16, i32 = jnp.float32, jnp.bfloat16, jnp.int32
 
 
@@ -29,30 +30,38 @@
     step = pl.program_id(0)
     left, d, keep = masks()
     eye = d == 0
+    eye_right = eye & ~left
     pairs = out_ref.shape[1] // 5
+    interiors = []
+    for q in range(STEP_FACES):
+        c = coupling_ref[q]
+        mid = c[:, Q : 2 * Q]
+        columns = jnp.concatenate([c[:, 2 * Q :], mid, mid, c[:, :Q]], axis=1)
+        face = step * STEP_FACES + q
+        interiors.append(
+            jnp.dot(
+                factors_ref[block_ref[face]], columns, preferred_element_type=f32
+            ).astype(bf16)
+        )
+    grams = [
+        lax.dot_general(x, x, (((0,), (0,)), ((), ())), preferred_element_type=f32)
+        for x in interiors
+    ]
     for pair in range(STEP_FACES // 2):
         last = None
         for odd in range(2):
             q = pair * 2 + odd
             face = step * STEP_FACES + q
-            c = coupling_ref[q]
-            mid = c[:, Q : 2 * Q]
-            columns = jnp.concatenate([c[:, 2 * Q :], mid, mid, c[:, :Q]], axis=1)
-            interior = jnp.dot(
-                factors_ref[block_ref[face]], columns, preferred_element_type=f32
-            ).astype(bf16)
-            g = lax.dot_general(
-                interior, interior, (((0,), (0,)), ((), ())), preferred_element_type=f32
-            )
+            g = grams[q]
             d3, r1 = g[:Q, :LANES], g[Q : 2 * Q, :LANES]
             t0, d1 = g[3 * Q :, :LANES], g[3 * Q :, LANES:]
             diag01 = diag_ref[q : q + 1, :LANES]
             diag2 = jnp.concatenate([diag_ref[q : q + 1, LANES:]] * 2, axis=1)
-            t1 = jnp.where(eye & ~left, swap_halves(diag01), 0.0) - jnp.where(
+            t1 = jnp.where(eye_right, swap_halves(diag01), 0.0) - jnp.where(
                 left | ~keep, r1, d1
             )
             d2_diag = jnp.sum(
-                jnp.where(eye & ~left, diag01 - r1, 0.0), axis=1, keepdims=True
+                jnp.where(eye_right, diag01 - r1, 0.0), axis=1, keepdims=True
             )
             spare = jnp.where(
                 d == KEEP,
@@ -103,7 +112,7 @@
             scratch_shapes=[pltpu.VMEM((5 * Q * pairs, LANES), f32)],
         ),
         out_shape=jax.ShapeDtypeStruct((Q, 5 * pairs, LANES), bf16),
-        compiler_params=pltpu.CompilerParams(vmem_limit_bytes=VMEM_LIMIT),
+        compiler_params=pltpu.CompilerParams(vmem_limit_bytes=PACK_VMEM),
         name="pack_faces",
     )(face_block, owner, slot, coupling, factors, face_diag)
 
@@ -230,17 +239,17 @@
         inner += lax.dot_general(
             part, rows_t, (((1,), (1,)), ((), ())), preferred_element_type=f32
         )
-    top = 0.0
+    upper = lower = 0.0
     for part in split3(inner):
-        top += jnp.dot(rows_t, part, preferred_element_type=f32)
-    size = top.shape[0]
-    for k in range(size // LANES):
-        top_ref[size * k : size * (k + 1), :] = top[:, LANES * k : LANES * (k + 1)]
+        upper += jnp.dot(rows_t[:LANES], part, preferred_element_type=f32)
+        lower += jnp.dot(rows_t[LANES:], part[:, LANES:], preferred_element_type=f32)
+    top_ref[:LANES, :] = upper[:, :LANES]
+    top_ref[LANES : 2 * LANES, :] = upper[:, LANES:]
+    top_ref[2 * LANES :, :] = lower
 
 
 def owned_and_top(z, basis, rows_t):
     slots, width, coarse = basis.shape
-    size = rows_t.shape[0]
     vmem = pl.BlockSpec(memory_space=pltpu.VMEM)
     return pl.pallas_call(
         coarse_kernel,
@@ -252,15 +261,53 @@
         ],
         out_shape=[
             jax.ShapeDtypeStruct((slots, width, width), bf16),
-            jax.ShapeDtypeStruct((size * size // LANES, LANES), f32),
+            jax.ShapeDtypeStruct((3 * LANES, LANES), f32),
         ],
         compiler_params=pltpu.CompilerParams(vmem_limit_bytes=VMEM_LIMIT),
         name="owned_and_top",
     )(z, basis, rows_t)
 
 
-def exchange(x, axis):
-    return lax.all_to_all(x, axis, split_axis=0, concat_axis=0, tiled=True)
+def mirror_kernel(x_ref, out_ref):
+    mid = x_ref[LANES : 2 * LANES, :]
+    out_ref[:LANES, :LANES] = x_ref[:LANES, :]
+    out_ref[:LANES, LANES:] = mid
+    out_ref[LANES:, :LANES] = mid.T
+    out_ref[LANES:, LANES:] = x_ref[2 * LANES :, :]
+
+
+def mirror(x):
+    return pl.pallas_call(
+        mirror_kernel,
+        in_specs=[pl.BlockSpec(memory_space=pltpu.VMEM)],
+        out_specs=pl.BlockSpec(memory_space=pltpu.VMEM),
+        out_shape=jax.ShapeDtypeStruct((2 * LANES, 2 * LANES), f32),
+        compiler_params=pltpu.CompilerParams(vmem_limit_bytes=VMEM_LIMIT),
+        name="mirror",
+    )(x)
+
+
+def exchange(x, axis, members=None):
+    return lax.all_to_all(
+        x, axis, split_axis=0, concat_axis=0, tiled=True, axis_index_groups=members
+    )
+
+
+def sum_over_all(x, axes):
+    peers, groups = (lax.axis_size(a) for a in axes[::-1])
+    near = 16
+    near_members = [[k * near + i for i in range(near)] for k in range(peers // near)]
+    far_members = [
+        list(range(i, peers * groups, near)) for i in range(near)
+    ]
+    far = peers * groups // near
+    rows = x.shape[0] // near
+    x = x.reshape(near, rows, LANES).astype(f32)
+    x = jnp.sum(exchange(x, "sub", near_members).astype(f32), axis=0).astype(bf16)
+    x = exchange(jnp.broadcast_to(x, (far, rows, LANES)), axes, far_members)
+    x = jnp.sum(x.astype(f32), axis=0).astype(f32)
+    x = exchange(jnp.broadcast_to(x, (near, rows, LANES)), "sub", near_members)
+    return x.reshape(near * rows, LANES).astype(f32)
 
 
 def local(
@@ -274,26 +321,17 @@
     coarse_index,
     projection,
 ):
-    peers, groups = lax.axis_size("sub"), lax.axis_size("grp")
     me = lax.axis_index("sub").astype(i32).reshape(1)
     x = pack_faces(face_block, face_owner[:, 0], owner_slot, coupling, factors, face_diag)
     x = exchange(x, "sub")
-    group_size, size = projection.shape
+    group_size = projection.shape[0]
     placement = (coarse_index[:, None] == lax.iota(i32, group_size)[None, :]).astype(bf16)
     rows_t = lax.dot_general(
         projection, placement, (((0,), (1,)), ((), ())), preferred_element_type=f32
     ).astype(bf16)
     z = exchange(merge_rows(me, x), "sub")
     owned, top = owned_and_top(z, coarse_basis, rows_t)
-    share = size * size // LANES // peers
-    part = jnp.sum(exchange(top.reshape(peers, share, LANES), "sub"), axis=0)
-    part = jnp.sum(
-        exchange(jnp.broadcast_to(part, (groups, share, LANES)), "grp"), axis=0
-    )
-    full = exchange(jnp.broadcast_to(part, (peers, share, LANES)), "sub")
-    full = full.reshape(size // LANES, size, LANES)
-    top_matrix = jnp.concatenate([full[k] for k in range(size // LANES)], axis=1)
-    return owned, top_matrix
+    return owned, mirror(sum_over_all(top, ("grp", "sub")))
 
 
 def solution(mesh):

time: 147 us -> 132 us (0.90)
  blocking collectives: 51.5 us -> 42 us
  Pallas kernels: 19.4 us -> 16 us
  local copies, waits for them, and re-layouts: 1.93 us -> 0.06 us
    all_to_all x3, blocking collectives: 51.5 us -> 42 us  [exchange(): lax.all_to_all(x, axis, split_axis=0, concat_axis=0, tiled=True, axis_ind...]
    unnamed x8 -> x6, local copies, waits for them, and re-layouts: 1.88 us -> 0.02 us
    pallas_call x1, Pallas kernels: 9.53 us -> 7.88 us  [pack_faces(): pl.pallas_call(schur_kernel, grid_spec=pltpu.PrefetchScalarGridSpec(num_s...]
  transfers between devices with their start and end apart: 2 -> 2, of which waited for: 2 -> 2; matrix products, arithmetic and copies ran while one was open for 1% -> 0% of each run, Pallas kernels for 0% -> 0%
where the time goes in v2:
time: 132 us; the launch traced here: 131 us
  waiting for transfers between devices  50.9 us (39%)
  blocking collectives  42 us (32%)
  starting transfers between devices  21.2 us (16%)
  Pallas kernels  16 us (12%)
    all_to_all x2, waiting for transfers between devices, exchange(): lax.all_to_all(x, axis, split_axis=0, concat_axis=0, tiled=True, axis_ind...  50.9 us
    all_to_all x3, blocking collectives, exchange(): lax.all_to_all(x, axis, split_axis=0, concat_axis=0, tiled=True, axis_ind...  42 us
    all_to_all x2, starting transfers between devices, exchange(): lax.all_to_all(x, axis, split_axis=0, concat_axis=0, tiled=True, axis_ind...  21.2 us
    pallas_call x1, Pallas kernels, pack_faces(): pl.pallas_call(schur_kernel, grid_spec=pltpu.PrefetchScalarGridSpec(num_s...  7.88 us
    pallas_call x1, Pallas kernels, merge_rows(): pl.pallas_call(merge_kernel, in_specs=[pl.BlockSpec(memory_space=pltpu.SM...  4.2 us
    pallas_call x1, Pallas kernels, owned_and_top(): pl.pallas_call(coarse_kernel, in_specs=[vmem, vmem, vmem], out_specs=[vme...  3.16 us
  transfers between devices with their start and end apart: 2, of which 2 were waited for; matrix products, arithmetic and copies ran while one was open for 0% of the time, Pallas kernels for 0%

profile of v2, /device:TPU:1, one launch (start us, length us, event | category | flops | bytes accessed | tf_op | source)
XLA Modules:
  0.0 131.3 jit_solution(12842011967809716389)
XLA Ops:
  0.6 0.0 copy-start
  0.6 7.9 %pack_faces.1 = bf16[64,80,128]{2,1,0:T(8,128)(2,1)} custom-call(s32[32]{0:T(128)} %block_ref.1, s32[32]{0:T(128)} %bitcast.9, s32[32]{0:T(128)} %slot_ref.1, bf16[32,192,192]{2,1,0:T(8,128)(2,1)} %coupling_ref.1, bf16[4,192,192]{2,1,0:T(8,128)(2,1)} %factors_ref.1, f32[32,192]{1,0:T(8,128)} %diag_ref.1), custom_call_target="tpu_custom_call" | custom-call | tf_op jit(solution)/shard_map/pack_faces/pallas_call | solution.py:101
  8.5 14.8 %all-to-all-start = ((bf16[64,80,128]{2,1,0:T(8,128)(2,1)}), bf16[64,80,128]{2,1,0:T(8,128)(2,1)S(1)}, u32[]{:S(2)}, u32[]{:S(2)}) async-start(bf16[64,80,128]{2,1,0:T(8,128)(2,1)} %pack_faces.1), calls=%async_computation | async-start | bytes 2621440 | tf_op jit(solution)/shard_map/all_to_all | solution.py:291
  23.4 33.6 %all-to-all-done.x_ref = bf16[64,80,128]{2,1,0:T(8,128)(2,1)S(1)} async-done(((bf16[64,80,128]{2,1,0:T(8,128)(2,1)}), bf16[64,80,128]{2,1,0:T(8,128)(2,1)S(1)}, u32[]{:S(2)}, u32[]{:S(2)}) %all-to-all-start) | async-done | bytes 1310752 | tf_op jit(solution)/shard_map/all_to_all | solution.py:291
  57.0 0.0 copy-start.2
  57.0 0.0 copy-start.1
  57.0 4.2 %merge_rows.1 = bf16[64,32,128]{2,1,0:T(8,128)(2,1)} custom-call(s32[1]{0:T(128)} %bitcast.me_ref, bf16[64,80,128]{2,1,0:T(8,128)(2,1)S(1)} %all-to-all-done.x_ref), custom_call_target="tpu_custom_call" | custom-call | tf_op jit(solution)/shard_map/merge_rows/pallas_call | solution.py:174
  61.2 6.3 %all-to-all-start.1 = ((bf16[64,32,128]{2,1,0:T(8,128)(2,1)}), bf16[64,32,128]{2,1,0:T(8,128)(2,1)S(1)}, u32[]{:S(2)}, u32[]{:S(2)}) async-start(bf16[64,32,128]{2,1,0:T(8,128)(2,1)} %merge_rows.1), calls=%async_computation.1 | async-start | bytes 1048576 | tf_op jit(solution)/shard_map/all_to_all | solution.py:291
  67.5 0.0 copy-done
  67.5 0.0 copy-done.2
  67.5 0.4 fusion.rows_ref
  67.9 17.3 %all-to-all-done.1.z_ref = bf16[64,32,128]{2,1,0:T(8,128)(2,1)S(1)} async-done(((bf16[64,32,128]{2,1,0:T(8,128)(2,1)}), bf16[64,32,128]{2,1,0:T(8,128)(2,1)S(1)}, u32[]{:S(2)}, u32[]{:S(2)}) %all-to-all-start.1) | async-done | bytes 524320 | tf_op jit(solution)/shard_map/all_to_all | solution.py:291
  85.2 0.0 copy-done.1
  85.2 3.2 %owned_and_top.1 = (bf16[12,192,192]{2,1,0:T(8,128)(2,1)}, f32[384,128]{1,0:T(8,128)S(1)}) custom-call(bf16[64,32,128]{2,1,0:T(8,128)(2,1)S(1)} %all-to-all-done.1.z_ref, bf16[12,192,128]{2,1,0:T(8,128)(2,1)S(1)} %copy-done.1, bf16[256,128]{1,0:T(8,128)(2,1)S(1)} %fusion.rows_ref), custom_call_target="tpu_custom_call" | custom-call | tf_op jit(solution)/shard_map/owned_and_top/pallas_call | solution.py:254
  88.4 11.2 %all_to_all.25 = f32[16,24,128]{2,1,0:T(8,128)S(1)} all-to-all(f32[16,24,128]{2,1,0:T(8,128)S(1)} %bitcast.8), channel_id=1, replica_groups={{0,1,2,3,4,5,6,7,8,9,10,11,12,13,14,15},{16,17,18,19,20,21,22,23,24,25,..., dimensions={0} | all-to-all | bytes 393216 | tf_op jit(solution)/shard_map/all_to_all | solution.py:291
  99.6 19.1 %all_to_all.26 = bf16[32,24,128]{2,1,0:T(8,128)(2,1)S(1)} all-to-all(bf16[32,24,128]{2,1,0:T(8,128)(2,1)S(1)} %broadcast_in_dim.8), channel_id=1, replica_groups={{0,16,32,48,64,80,96,112,128,144,160,176,192,208,224,240,256,272,288,30..., dimensions={0} | all-to-all | bytes 393216 | tf_op jit(solution)/shard_map/all_to_all | solution.py:291
  118.8 11.8 %all_to_all.27 = f32[16,24,128]{2,1,0:T(8,128)S(1)} all-to-all(f32[16,24,128]{2,1,0:T(8,128)S(1)} %broadcast_in_dim.9), channel_id=1, replica_groups={{0,1,2,3,4,5,6,7,8,9,10,11,12,13,14,15},{16,17,18,19,20,21,22,23,24,25,..., dimensions={0} | all-to-all | bytes 393216 | tf_op jit(solution)/shard_map/all_to_all | solution.py:291
  130.5 0.8 mirror.1
  (4 shorter events, 0.1 us)
Async XLA Ops:
  0.6 66.9 %copy-start = (bf16[768,256]{1,0:T(8,128)(2,1)S(1)}, bf16[768,256]{1,0:T(8,128)(2,1)}, u32[]{:S(2)}) copy-start(bf16[768,256]{1,0:T(8,128)(2,1)} %param.17) | copy-start | bytes 1179652
  8.5 48.5 %all-to-all-start = ((bf16[64,80,128]{2,1,0:T(8,128)(2,1)}), bf16[64,80,128]{2,1,0:T(8,128)(2,1)S(1)}, u32[]{:S(2)}, u32[]{:S(2)}) async-start(bf16[64,80,128]{2,1,0:T(8,128)(2,1)} %pack_faces.1), calls=%async_computation | async-start | bytes 2621440 | tf_op jit(solution)/shard_map/all_to_all | solution.py:291
  57.0 10.5 %copy-start.2 = (s32[128]{0:T(128)S(1)}, s32[128]{0:T(128)}, u32[]{:S(2)}) copy-start(s32[128]{0:T(128)} %param.16) | copy-start | bytes 1540
  57.0 28.2 %copy-start.1 = (bf16[12,192,128]{2,1,0:T(8,128)(2,1)S(1)}, bf16[12,192,128]{2,1,0:T(8,128)(2,1)}, u32[]{:S(2)}) copy-start(bf16[12,192,128]{2,1,0:T(8,128)(2,1)} %basis_ref.1) | copy-start | bytes 1769476
  61.2 24.0 %all-to-all-start.1 = ((bf16[64,32,128]{2,1,0:T(8,128)(2,1)}), bf16[64,32,128]{2,1,0:T(8,128)(2,1)S(1)}, u32[]{:S(2)}, u32[]{:S(2)}) async-start(bf16[64,32,128]{2,1,0:T(8,128)(2,1)} %merge_rows.1), calls=%async_computation.1 | async-start | bytes 1048576 | tf_op jit(solution)/shard_map/all_to_all | solution.py:291

commit v3 on v2

--- a/solution.py
+++ b/solution.py
@@ -26,43 +26,81 @@
     return pltpu.roll(x, Q, 1)
 
 
-def schur_kernel(block_ref, owner_ref, slot_ref, coupling_ref, factors_ref, diag_ref, out_ref, scratch):
-    step = pl.program_id(0)
+def schur_kernel(
+    block_hbm,
+    owner_hbm,
+    slot_hbm,
+    coupling_hbm,
+    factors_hbm,
+    diag_hbm,
+    out_ref,
+    scratch,
+    coupling_ref,
+    factors_ref,
+    diag_ref,
+    block_ref,
+    owner_ref,
+    slot_ref,
+    sems,
+):
+    faces = coupling_ref.shape[0]
+    steps = faces // STEP_FACES
+    pairs = faces // 2
+    copies = [
+        pltpu.make_async_copy(block_hbm, block_ref, sems.at[0]),
+        pltpu.make_async_copy(factors_hbm, factors_ref, sems.at[1]),
+    ]
+    for s in range(steps):
+        part = pl.ds(s * STEP_FACES, STEP_FACES)
+        copies.append(
+            pltpu.make_async_copy(
+                coupling_hbm.at[part], coupling_ref.at[part], sems.at[2 + s]
+            )
+        )
+    copies += [
+        pltpu.make_async_copy(diag_hbm, diag_ref, sems.at[2 + steps]),
+        pltpu.make_async_copy(owner_hbm, owner_ref, sems.at[3 + steps]),
+        pltpu.make_async_copy(slot_hbm, slot_ref, sems.at[4 + steps]),
+    ]
+    for copy in copies:
+        copy.start()
     left, d, keep = masks()
     eye = d == 0
     eye_right = eye & ~left
-    pairs = out_ref.shape[1] // 5
-    interiors = []
-    for q in range(STEP_FACES):
-        c = coupling_ref[q]
-        mid = c[:, Q : 2 * Q]
-        columns = jnp.concatenate([c[:, 2 * Q :], mid, mid, c[:, :Q]], axis=1)
-        face = step * STEP_FACES + q
-        interiors.append(
-            jnp.dot(
-                factors_ref[block_ref[face]], columns, preferred_element_type=f32
-            ).astype(bf16)
-        )
-    grams = [
-        lax.dot_general(x, x, (((0,), (0,)), ((), ())), preferred_element_type=f32)
-        for x in interiors
-    ]
-    for pair in range(STEP_FACES // 2):
+    copies[0].wait()
+    copies[1].wait()
+    for s in range(steps):
+        copies[2 + s].wait()
+        interiors = []
+        for face in range(s * STEP_FACES, (s + 1) * STEP_FACES):
+            c = coupling_ref[face]
+            mid = c[:, Q : 2 * Q]
+            columns = jnp.concatenate([c[:, 2 * Q :], mid, mid, c[:, :Q]], axis=1)
+            interiors.append(
+                jnp.dot(
+                    factors_ref[block_ref[face]], columns, preferred_element_type=f32
+                ).astype(bf16)
+            )
+        grams = [
+            lax.dot_general(x, x, (((0,), (0,)), ((), ())), preferred_element_type=f32)
+            for x in interiors
+        ]
+        if s == 0:
+            for copy in copies[-3:]:
+                copy.wait()
         last = None
-        for odd in range(2):
-            q = pair * 2 + odd
-            face = step * STEP_FACES + q
-            g = grams[q]
+        for q, g in enumerate(grams):
+            face = s * STEP_FACES + q
             d3, r1 = g[:Q, :LANES], g[Q : 2 * Q, :LANES]
             t0, d1 = g[3 * Q :, :LANES], g[3 * Q :, LANES:]
-            diag01 = diag_ref[q : q + 1, :LANES]
-            diag2 = jnp.concatenate([diag_ref[q : q + 1, LANES:]] * 2, axis=1)
-            t1 = jnp.where(eye_right, swap_halves(diag01), 0.0) - jnp.where(
+            diag01 = diag_ref[face : face + 1, :LANES]
+            diag2 = jnp.concatenate([diag_ref[face : face + 1, LANES:]] * 2, axis=1)
+            diag10 = swap_halves(diag01)
+            t1 = jnp.where(eye_right, diag10, 0.0) - jnp.where(
                 left | ~keep, r1, d1
             )
-            d2_diag = jnp.sum(
-                jnp.where(eye_right, diag01 - r1, 0.0), axis=1, keepdims=True
-            )
+            r2 = g[Q : 2 * Q, LANES:]
+            d2_diag = diag10 - pltpu.roll(r2, 1, 0)
             spare = jnp.where(
                 d == KEEP,
                 d2_diag,
@@ -73,44 +111,39 @@
                 ),
             )
             f = jnp.where(keep, jnp.where(eye, diag2, 0.0) - d3, spare)
-            at = step * (STEP_FACES // 2) + pair
 
             def put(k, value):
-                scratch[pl.ds(k * Q * pairs + at, Q, stride=pairs), :] = value
-
+                scratch[pl.ds(k * Q * (pairs + 1) + face // 2, Q, stride=pairs + 1), :] = value
+
+            odd = face % 2
             put(2 * odd, -t0)
             put(2 * odd + 1, t1)
             if odd:
                 put(4, jnp.where(left, last, swap_halves(f)))
             last = f
-
-    @pl.when(step == pl.num_programs(0) - 1)
-    def _():
-        for k in range(5):
-            out_ref[:, pairs * k : pairs * (k + 1), :] = (
-                scratch[Q * pairs * k : Q * pairs * (k + 1), :]
-                .reshape(Q, pairs, LANES)
-                .astype(bf16)
-            )
+    for k in range(5):
+        for j in range(Q):
+            at = Q * (pairs + 1) * k + (pairs + 1) * j
+            out_ref[j, pairs * k : pairs * (k + 1), :] = scratch[at : at + pairs, :].astype(bf16)
 
 
 def pack_faces(face_block, owner, slot, coupling, factors, face_diag):
-    faces, width, _ = coupling.shape
-    blocks = factors.shape[0]
+    faces = coupling.shape[0]
     pairs = faces // 2
     return pl.pallas_call(
         schur_kernel,
-        grid_spec=pltpu.PrefetchScalarGridSpec(
-            num_scalar_prefetch=3,
-            grid=(faces // STEP_FACES,),
-            in_specs=[
-                pl.BlockSpec((STEP_FACES, width, width), lambda s, *_: (s, 0, 0)),
-                pl.BlockSpec((blocks, width, width), lambda s, *_: (0, 0, 0)),
-                pl.BlockSpec((STEP_FACES, width), lambda s, *_: (s, 0)),
-            ],
-            out_specs=pl.BlockSpec((Q, 5 * pairs, LANES), lambda s, *_: (0, 0, 0)),
-            scratch_shapes=[pltpu.VMEM((5 * Q * pairs, LANES), f32)],
-        ),
+        in_specs=[pl.BlockSpec(memory_space=pl.ANY)] * 6,
+        out_specs=pl.BlockSpec(memory_space=pltpu.VMEM),
+        scratch_shapes=[
+            pltpu.VMEM((5 * Q * (pairs + 1), LANES), f32),
+            pltpu.VMEM(coupling.shape, bf16),
+            pltpu.VMEM(factors.shape, bf16),
+            pltpu.VMEM(face_diag.shape, f32),
+            pltpu.SMEM((faces,), i32),
+            pltpu.SMEM((faces,), i32),
+            pltpu.SMEM((faces,), i32),
+            pltpu.SemaphoreType.DMA((5 + faces // STEP_FACES,)),
+        ],
         out_shape=jax.ShapeDtypeStruct((Q, 5 * pairs, LANES), bf16),
         compiler_params=pltpu.CompilerParams(vmem_limit_bytes=PACK_VMEM),
         name="pack_faces",
@@ -137,15 +170,24 @@
     named = lax.dot_general(
         pick, shared, (((1,), (1,)), ((), ())), preferred_element_type=f32
     ).astype(i32)
-    target = lax.broadcasted_iota(i32, (slots * peers, total), 0)
-    even = (target == named[1:2] * peers + named[0:1]).astype(f32).astype(bf16)
-    odd = (target == named[3:4] * peers + named[2:3]).astype(f32).astype(bf16)
-    sums = []
+    owners = lax.broadcasted_iota(i32, (peers, total), 0)
+    hots = []
     for k in range(2):
-        sums.append(
-            jnp.dot(even, piece(k), preferred_element_type=f32)
-            + jnp.dot(odd, piece(2 + k), preferred_element_type=f32)
+        owner_hot = (owners == named[2 * k : 2 * k + 1]).astype(f32).astype(bf16)
+        slot = named[2 * k + 1 : 2 * k + 2]
+        hots.append(
+            jnp.concatenate(
+                [owner_hot * (slot == s).astype(f32).astype(bf16) for s in range(slots)],
+                axis=0,
+            )
         )
+    even, odd = hots
+    both = jnp.dot(
+        even, jnp.concatenate([piece(0), piece(1)], axis=1), preferred_element_type=f32
+    ) + jnp.dot(
+        odd, jnp.concatenate([piece(2), piece(3)], axis=1), preferred_element_type=f32
+    )
+    sums = [both[:, :LANES], both[:, LANES:]]
     low = jnp.dot(even, shared, preferred_element_type=f32)
     high = jnp.dot(odd, shared, preferred_element_type=f32)
     half = slots // 2
@@ -161,12 +203,14 @@
     out_rows = out_ref.shape[1]
     for k in range(3):
         for s in range(sums[k].shape[0] // peers):
-            flat[pl.ds(slots * k + s, peers, stride=out_rows), :] = sums[k][
+            flat[pl.ds(slots * k + s, peers, stride=out_rows + 1), :] = sums[k][
                 peers * s : peers * (s + 1), :
             ]
     for s in range(slots * 2 + half, out_rows):
-        flat[pl.ds(s, peers, stride=out_rows), :] = jnp.zeros((peers, LANES), f32)
-    out_ref[...] = flat[...].reshape(peers, out_rows, LANES).astype(bf16)
+        flat[pl.ds(s, peers, stride=out_rows + 1), :] = jnp.zeros((peers, LANES), f32)
+    for j in range(peers):
+        at = (out_rows + 1) * j
+        out_ref[j] = flat[at : at + out_rows, :].astype(bf16)
 
 
 def merge_rows(me, x):
@@ -178,7 +222,7 @@
             pl.BlockSpec(memory_space=pltpu.VMEM),
         ],
         out_specs=pl.BlockSpec(memory_space=pltpu.VMEM),
-        scratch_shapes=[pltpu.VMEM((peers * 32, LANES), f32)],
+        scratch_shapes=[pltpu.VMEM((peers * 33, LANES), f32)],
         out_shape=jax.ShapeDtypeStruct((peers, 32, LANES), bf16),
         compiler_params=pltpu.CompilerParams(vmem_limit_bytes=VMEM_LIMIT),
         name="merge_rows",
@@ -192,28 +236,30 @@
     return a, b, (rest - b.astype(f32)).astype(bf16)
 
 
-def coarse_kernel(z_ref, basis_ref, rows_ref, owned_ref, top_ref, flat, applied):
+def coarse_kernel(
+    z_ref, basis_ref, rows_ref, owned_hbm, top_ref, flat, applied, owned_ref, sems
+):
     slots, width, coarse = basis_ref.shape
     half = slots // 2
-    step = z_ref.shape[1]
+    rows = z_ref.shape[1]
+    step = rows + 1
     left, d, keep = masks()
     eye = d == 0
-    flat[...] = z_ref[...].reshape(Q * step, LANES).astype(f32)
+    for j in range(Q):
+        flat[step * j : step * j + rows, :] = z_ref[j].astype(f32)
     for q in range(half):
         f_both = flat[pl.ds(slots * 2 + q, Q, stride=step), :]
         f_turned = f_both.T
+        moved = pltpu.roll(f_both, Q - 1, 0)
         for r in (q, q + half):
             t0 = flat[pl.ds(r, Q, stride=step), :]
             t1 = flat[pl.ds(slots + r, Q, stride=step), :]
             turned = jnp.concatenate([t0, t1], axis=0).T
             lower = turned[Q:]
             if r == q:
-                f, f_t = f_both, f_turned[:Q]
+                f, f_t, d2_diag = f_both, f_turned[:Q], swap_halves(moved)
             else:
-                f, f_t = swap_halves(f_both), f_turned[Q:]
-            d2_diag = jnp.sum(
-                jnp.where((d == KEEP) & left, f, 0.0), axis=1, keepdims=True
-            )
+                f, f_t, d2_diag = swap_halves(f_both), f_turned[Q:], moved
             d1 = swap_halves(jnp.where(keep, t1, lower))
             d2 = jnp.where(eye, d2_diag, jnp.where(keep, lower, t1))
             d3 = jnp.where(keep[:, :Q], f[:, :Q], f_t)
@@ -223,14 +269,19 @@
             owned_ref[r, Q : 2 * Q, LANES:] = t1[:, :Q].astype(bf16)
             owned_ref[r, 2 * Q :, :LANES] = turned[:Q].astype(bf16)
             owned_ref[r, 2 * Q :, LANES:] = d3.astype(bf16)
+    copies = [
+        pltpu.make_async_copy(owned_ref.at[r], owned_hbm.at[r], sems.at[r])
+        for r in range(slots)
+    ]
+    for copy in copies:
+        copy.start()
     for r in range(slots):
         applied[r] = jnp.dot(
             owned_ref[r], basis_ref[r], preferred_element_type=f32
         ).astype(bf16)
-    local_coarse = lax.dot_general(
-        basis_ref[...].reshape(slots * width, coarse),
+    local_coarse = jnp.dot(
+        basis_ref[...].reshape(slots * width, coarse).T,
         applied[...].reshape(slots * width, coarse),
-        (((0,), (0,)), ((), ())),
         preferred_element_type=f32,
     )
     rows_t = rows_ref[...]
@@ -246,6 +297,8 @@
     top_ref[:LANES, :] = upper[:, :LANES]
     top_ref[LANES : 2 * LANES, :] = upper[:, LANES:]
     top_ref[2 * LANES :, :] = lower
+    for copy in copies:
+        copy.wait()
 
 
 def owned_and_top(z, basis, rows_t):
@@ -253,11 +306,13 @@
     vmem = pl.BlockSpec(memory_space=pltpu.VMEM)
     return pl.pallas_call(
         coarse_kernel,
-        in_specs=[vmem, vmem, vmem],
-        out_specs=[vmem, vmem],
+        in_specs=[vmem] * 3,
+        out_specs=[pl.BlockSpec(memory_space=pltpu.HBM), vmem],
         scratch_shapes=[
-            pltpu.VMEM((Q * z.shape[1], LANES), f32),
+            pltpu.VMEM((Q * (z.shape[1] + 1), LANES), f32),
             pltpu.VMEM((slots, width, coarse), bf16),
+            pltpu.VMEM((slots, width, width), bf16),
+            pltpu.SemaphoreType.DMA((slots,)),
         ],
         out_shape=[
             jax.ShapeDtypeStruct((slots, width, width), bf16),
@@ -302,7 +357,7 @@
     ]
     far = peers * groups // near
     rows = x.shape[0] // near
-    x = x.reshape(near, rows, LANES).astype(f32)
+    x = x.reshape(near, rows, LANES).astype(bf16)
     x = jnp.sum(exchange(x, "sub", near_members).astype(f32), axis=0).astype(bf16)
     x = exchange(jnp.broadcast_to(x, (far, rows, LANES)), axes, far_members)
     x = jnp.sum(x.astype(f32), axis=0).astype(f32)
@@ -325,11 +380,12 @@
     x = pack_faces(face_block, face_owner[:, 0], owner_slot, coupling, factors, face_diag)
     x = exchange(x, "sub")
     group_size = projection.shape[0]
+    z = exchange(merge_rows(me, x), "sub")
+    z, coarse_index = lax.optimization_barrier((z, coarse_index))
     placement = (coarse_index[:, None] == lax.iota(i32, group_size)[None, :]).astype(bf16)
     rows_t = lax.dot_general(
         projection, placement, (((0,), (1,)), ((), ())), preferred_element_type=f32
     ).astype(bf16)
-    z = exchange(merge_rows(me, x), "sub")
     owned, top = owned_and_top(z, coarse_basis, rows_t)
     return owned, mirror(sum_over_all(top, ("grp", "sub")))
 

time: 132 us -> 126 us (0.955)
  blocking collectives: 42 us -> 64.8 us
  waiting for transfers between devices: 50.9 us -> 33.6 us
  starting transfers between devices: 21.2 us -> 14.8 us
  Pallas kernels: 16 us -> 11.2 us
    all_to_all x3 -> x4, blocking collectives: 42 us -> 64.8 us  [exchange(): lax.all_to_all(x, axis, split_axis=0, concat_axis=0, tiled=True, axis_ind...]
    all_to_all x2 -> x1, waiting for transfers between devices: 50.9 us -> 33.6 us  [exchange(): lax.all_to_all(x, axis, split_axis=0, concat_axis=0, tiled=True, axis_ind...]
    all_to_all x2 -> x1, starting transfers between devices: 21.2 us -> 14.8 us  [exchange(): lax.all_to_all(x, axis, split_axis=0, concat_axis=0, tiled=True, axis_ind...]
    pallas_call x2, Pallas kernels: 11 us -> 8.38 us  [the longest x1 5.8 us: pack_faces(): pl.pallas_call(schur_kernel, in_specs=[pl.BlockSpec(memory_space=pl.ANY)]...]
    pallas_call x1, Pallas kernels: 4.2 us -> 1.97 us  [merge_rows(): pl.pallas_call(merge_kernel, in_specs=[pl.BlockSpec(memory_space=pltpu.SM...]
  transfers between devices with their start and end apart: 2 -> 1, of which waited for: 2 -> 1; matrix products, arithmetic and copies ran while one was open for 0% -> 0% of each run, Pallas kernels for 0% -> 0%
where the time goes in v3:
time: 126 us
  blocking collectives  64.8 us (51%)
  waiting for transfers between devices  33.6 us (27%)
  starting transfers between devices  14.8 us (12%)
  Pallas kernels  11.2 us (9%)
    all_to_all x4, blocking collectives, exchange(): lax.all_to_all(x, axis, split_axis=0, concat_axis=0, tiled=True, axis_ind...  64.8 us
    all_to_all x1, waiting for transfers between devices, exchange(): lax.all_to_all(x, axis, split_axis=0, concat_axis=0, tiled=True, axis_ind...  33.6 us
    all_to_all x1, starting transfers between devices, exchange(): lax.all_to_all(x, axis, split_axis=0, concat_axis=0, tiled=True, axis_ind...  14.8 us
    pallas_call x1, Pallas kernels, pack_faces(): pl.pallas_call(schur_kernel, in_specs=[pl.BlockSpec(memory_space=pl.ANY)]...  5.8 us
    pallas_call x1, Pallas kernels, owned_and_top(): pl.pallas_call(coarse_kernel, in_specs=[vmem] * 3, out_specs=[pl.BlockSpe...  2.58 us
  transfers between devices with their start and end apart: 1, of which 1 were waited for; matrix products, arithmetic and copies ran while one was open for 0% of the time, Pallas kernels for 0%

profile of v3, /device:TPU:1, one launch (start us, length us, event | category | flops | bytes accessed | tf_op | source)
XLA Modules:
  0.0 125.6 jit_solution(7576619662908286843)
XLA Ops:
  0.6 0.0 copy-start
  0.6 5.8 %pack_faces.1 = bf16[64,80,128]{2,1,0:T(8,128)(2,1)} custom-call(s32[32]{0:T(128)} %block_hbm.1, s32[32]{0:T(128)} %bitcast.9, s32[32]{0:T(128)} %slot_hbm.1, bf16[32,192,192]{2,1,0:T(8,128)(2,1)} %coupling_hbm.1, bf16[4,192,192]{2,1,0:T(8,128)(2,1)} %factors_hbm.1, f32[32,192]{1,0:T(8,128)} %diag_hbm.1), custom_call_target="tpu_custom_call" | custom-call | tf_op jit(solution)/shard_map/pack_faces/pallas_call | solution.py:133
  6.5 14.8 %all-to-all-start = ((bf16[64,80,128]{2,1,0:T(8,128)(2,1)}), bf16[64,80,128]{2,1,0:T(8,128)(2,1)S(1)}, u32[]{:S(2)}, u32[]{:S(2)}) async-start(bf16[64,80,128]{2,1,0:T(8,128)(2,1)} %pack_faces.1), calls=%async_computation | async-start | bytes 2621440 | tf_op jit(solution)/shard_map/all_to_all | solution.py:346
  21.3 33.6 %all-to-all-done.x_ref = bf16[64,80,128]{2,1,0:T(8,128)(2,1)S(1)} async-done(((bf16[64,80,128]{2,1,0:T(8,128)(2,1)}), bf16[64,80,128]{2,1,0:T(8,128)(2,1)S(1)}, u32[]{:S(2)}, u32[]{:S(2)}) %all-to-all-start) | async-done | bytes 1310752 | tf_op jit(solution)/shard_map/all_to_all | solution.py:346
  54.9 0.0 copy-start.2
  54.9 0.0 copy-start.1
  54.9 2.0 %merge_rows.1 = bf16[64,32,128]{2,1,0:T(8,128)(2,1)S(1)} custom-call(s32[1]{0:T(128)} %bitcast.me_ref, bf16[64,80,128]{2,1,0:T(8,128)(2,1)S(1)} %all-to-all-done.x_ref), custom_call_target="tpu_custom_call" | custom-call | tf_op jit(solution)/shard_map/merge_rows/pallas_call | solution.py:218
  56.9 23.8 %all_to_all.25.z_ref = bf16[64,32,128]{2,1,0:T(8,128)(2,1)S(1)} all-to-all(bf16[64,32,128]{2,1,0:T(8,128)(2,1)S(1)} %merge_rows.1), channel_id=1, replica_groups=mesh['grp'=8,'sub'=64] {'sub'}, dimensions={0} | all-to-all | bytes 1048576 | tf_op jit(solution)/shard_map/all_to_all | solution.py:346
  80.7 0.0 copy-done
  80.7 0.0 copy-done.2
  80.7 0.4 fusion.rows_ref
  81.1 0.0 copy-done.1
  81.1 2.6 %owned_and_top.1 = (bf16[12,192,192]{2,1,0:T(8,128)(2,1)}, f32[384,128]{1,0:T(8,128)S(1)}) custom-call(bf16[64,32,128]{2,1,0:T(8,128)(2,1)S(1)} %all_to_all.25.z_ref, bf16[12,192,128]{2,1,0:T(8,128)(2,1)S(1)} %copy-done.1, bf16[256,128]{1,0:T(8,128)(2,1)S(1)} %fusion.rows_ref), custom_call_target="tpu_custom_call" | custom-call | tf_op jit(solution)/shard_map/owned_and_top/pallas_call | solution.py:307
  83.7 10.4 %all_to_all.26 = bf16[16,24,128]{2,1,0:T(8,128)(2,1)S(1)} all-to-all(bf16[16,24,128]{2,1,0:T(8,128)(2,1)S(1)} %bitcast.8), channel_id=1, replica_groups={{0,1,2,3,4,5,6,7,8,9,10,11,12,13,14,15},{16,17,18,19,20,21,22,23,24,25,..., dimensions={0} | all-to-all | bytes 196608 | tf_op jit(solution)/shard_map/all_to_all | solution.py:346
  94.2 19.1 %all_to_all.27 = bf16[32,24,128]{2,1,0:T(8,128)(2,1)S(1)} all-to-all(bf16[32,24,128]{2,1,0:T(8,128)(2,1)S(1)} %broadcast_in_dim.8), channel_id=1, replica_groups={{0,16,32,48,64,80,96,112,128,144,160,176,192,208,224,240,256,272,288,30..., dimensions={0} | all-to-all | bytes 393216 | tf_op jit(solution)/shard_map/all_to_all | solution.py:346
  113.3 11.5 %all_to_all.28 = f32[16,24,128]{2,1,0:T(8,128)S(1)} all-to-all(f32[16,24,128]{2,1,0:T(8,128)S(1)} %broadcast_in_dim.9), channel_id=1, replica_groups={{0,1,2,3,4,5,6,7,8,9,10,11,12,13,14,15},{16,17,18,19,20,21,22,23,24,25,..., dimensions={0} | all-to-all | bytes 393216 | tf_op jit(solution)/shard_map/all_to_all | solution.py:346
  124.8 0.8 mirror.1
  (5 shorter events, 0.1 us)
Async XLA Ops:
  0.6 80.1 %copy-start = (bf16[768,256]{1,0:T(8,128)(2,1)S(1)}, bf16[768,256]{1,0:T(8,128)(2,1)}, u32[]{:S(2)}) copy-start(bf16[768,256]{1,0:T(8,128)(2,1)} %param.17) | copy-start | bytes 1179652
  6.5 48.5 %all-to-all-start = ((bf16[64,80,128]{2,1,0:T(8,128)(2,1)}), bf16[64,80,128]{2,1,0:T(8,128)(2,1)S(1)}, u32[]{:S(2)}, u32[]{:S(2)}) async-start(bf16[64,80,128]{2,1,0:T(8,128)(2,1)} %pack_faces.1), calls=%async_computation | async-start | bytes 2621440 | tf_op jit(solution)/shard_map/all_to_all | solution.py:346
  54.9 25.8 %copy-start.2 = (s32[128]{0:T(128)S(1)}, s32[128]{0:T(128)}, u32[]{:S(2)}) copy-start(s32[128]{0:T(128)} %param.16) | copy-start | bytes 1540
  54.9 26.2 %copy-start.1 = (bf16[12,192,128]{2,1,0:T(8,128)(2,1)S(1)}, bf16[12,192,128]{2,1,0:T(8,128)(2,1)}, u32[]{:S(2)}) copy-start(bf16[12,192,128]{2,1,0:T(8,128)(2,1)} %basis_ref.1) | copy-start | bytes 1769476

commit v4 on v3

--- a/solution.py
+++ b/solution.py
@@ -360,7 +360,7 @@
     x = x.reshape(near, rows, LANES).astype(bf16)
     x = jnp.sum(exchange(x, "sub", near_members).astype(f32), axis=0).astype(bf16)
     x = exchange(jnp.broadcast_to(x, (far, rows, LANES)), axes, far_members)
-    x = jnp.sum(x.astype(f32), axis=0).astype(f32)
+    x = jnp.sum(x.astype(f32), axis=0).astype(bf16)
     x = exchange(jnp.broadcast_to(x, (near, rows, LANES)), "sub", near_members)
     return x.reshape(near * rows, LANES).astype(f32)
 
@@ -380,12 +380,12 @@
     x = pack_faces(face_block, face_owner[:, 0], owner_slot, coupling, factors, face_diag)
     x = exchange(x, "sub")
     group_size = projection.shape[0]
-    z = exchange(merge_rows(me, x), "sub")
-    z, coarse_index = lax.optimization_barrier((z, coarse_index))
     placement = (coarse_index[:, None] == lax.iota(i32, group_size)[None, :]).astype(bf16)
     rows_t = lax.dot_general(
         projection, placement, (((0,), (1,)), ((), ())), preferred_element_type=f32
     ).astype(bf16)
+    x, rows_t = lax.optimization_barrier((x, rows_t))
+    z = exchange(merge_rows(me, x), "sub")
     owned, top = owned_and_top(z, coarse_basis, rows_t)
     return owned, mirror(sum_over_all(top, ("grp", "sub")))
 

time: 126 us -> 125 us (level)
  no operation moved by 1% of the time
where the time goes in v4:
time: 125 us; the launch traced here: 124 us
  blocking collectives  64 us (51%)
  waiting for transfers between devices  33.2 us (27%)
  starting transfers between devices  14.8 us (12%)
  Pallas kernels  11.2 us (9%)
    all_to_all x4, blocking collectives, exchange(): lax.all_to_all(x, axis, split_axis=0, concat_axis=0, tiled=True, axis_ind...  64 us
    all_to_all x1, waiting for transfers between devices, exchange(): lax.all_to_all(x, axis, split_axis=0, concat_axis=0, tiled=True, axis_ind...  33.2 us
    all_to_all x1, starting transfers between devices, exchange(): lax.all_to_all(x, axis, split_axis=0, concat_axis=0, tiled=True, axis_ind...  14.8 us
    pallas_call x1, Pallas kernels, pack_faces(): pl.pallas_call(schur_kernel, in_specs=[pl.BlockSpec(memory_space=pl.ANY)]...  5.8 us
    pallas_call x1, Pallas kernels, owned_and_top(): pl.pallas_call(coarse_kernel, in_specs=[vmem] * 3, out_specs=[pl.BlockSpe...  2.59 us
  transfers between devices with their start and end apart: 1, of which 1 were waited for; matrix products, arithmetic and copies ran while one was open for 0% of the time, Pallas kernels for 0%

profile of v4, /device:TPU:1, one launch (start us, length us, event | category | flops | bytes accessed | tf_op | source)
XLA Modules:
  0.0 124.4 jit_solution(5067214224433004739)
XLA Ops:
  0.6 0.0 copy-start
  0.6 5.8 %pack_faces.1 = bf16[64,80,128]{2,1,0:T(8,128)(2,1)} custom-call(s32[32]{0:T(128)} %block_hbm.1, s32[32]{0:T(128)} %bitcast.10, s32[32]{0:T(128)} %slot_hbm.1, bf16[32,192,192]{2,1,0:T(8,128)(2,1)} %coupling_hbm.1, bf16[4,192,192]{2,1,0:T(8,128)(2,1)} %factors_hbm.1, f32[32,192]{1,0:T(8,128)} %diag_hbm.1), custom_call_target="tpu_custom_call" | custom-call | tf_op jit(solution)/shard_map/pack_faces/pallas_call | solution.py:133
  6.5 0.0 copy-start.2
  6.5 14.8 %all-to-all-start = ((bf16[64,80,128]{2,1,0:T(8,128)(2,1)}), bf16[64,80,128]{2,1,0:T(8,128)(2,1)S(1)}, u32[]{:S(2)}, u32[]{:S(2)}) async-start(bf16[64,80,128]{2,1,0:T(8,128)(2,1)} %pack_faces.1), calls=%async_computation | async-start | bytes 2621440 | tf_op jit(solution)/shard_map/all_to_all | solution.py:346
  21.3 0.0 copy-done
  21.3 0.0 copy-done.2
  21.3 0.4 fusion.rows_ref
  21.7 33.2 %all-to-all-done.x_ref = bf16[64,80,128]{2,1,0:T(8,128)(2,1)S(1)} async-done(((bf16[64,80,128]{2,1,0:T(8,128)(2,1)}), bf16[64,80,128]{2,1,0:T(8,128)(2,1)S(1)}, u32[]{:S(2)}, u32[]{:S(2)}) %all-to-all-start) | async-done | bytes 1310752 | tf_op jit(solution)/shard_map/all_to_all | solution.py:346
  54.9 0.0 copy-start.1
  54.9 2.0 %merge_rows.1 = bf16[64,32,128]{2,1,0:T(8,128)(2,1)S(1)} custom-call(s32[1]{0:T(128)} %bitcast.me_ref, bf16[64,80,128]{2,1,0:T(8,128)(2,1)S(1)} %all-to-all-done.x_ref), custom_call_target="tpu_custom_call" | custom-call | tf_op jit(solution)/shard_map/merge_rows/pallas_call | solution.py:218
  56.9 23.8 %all_to_all.25.z_ref = bf16[64,32,128]{2,1,0:T(8,128)(2,1)S(1)} all-to-all(bf16[64,32,128]{2,1,0:T(8,128)(2,1)S(1)} %merge_rows.1), channel_id=1, replica_groups=mesh['grp'=8,'sub'=64] {'sub'}, dimensions={0} | all-to-all | bytes 1048576 | tf_op jit(solution)/shard_map/all_to_all | solution.py:346
  80.7 0.0 copy-done.1
  80.7 2.6 %owned_and_top.1 = (bf16[12,192,192]{2,1,0:T(8,128)(2,1)}, f32[384,128]{1,0:T(8,128)S(1)}) custom-call(bf16[64,32,128]{2,1,0:T(8,128)(2,1)S(1)} %all_to_all.25.z_ref, bf16[12,192,128]{2,1,0:T(8,128)(2,1)S(1)} %copy-done.1, bf16[256,128]{1,0:T(8,128)(2,1)S(1)} %fusion.rows_ref), custom_call_target="tpu_custom_call" | custom-call | tf_op jit(solution)/shard_map/owned_and_top/pallas_call | solution.py:307
  83.4 10.4 %all_to_all.26 = bf16[16,24,128]{2,1,0:T(8,128)(2,1)S(1)} all-to-all(bf16[16,24,128]{2,1,0:T(8,128)(2,1)S(1)} %bitcast.9), channel_id=1, replica_groups={{0,1,2,3,4,5,6,7,8,9,10,11,12,13,14,15},{16,17,18,19,20,21,22,23,24,25,..., dimensions={0} | all-to-all | bytes 196608 | tf_op jit(solution)/shard_map/all_to_all | solution.py:346
  93.8 19.1 %all_to_all.27 = bf16[32,24,128]{2,1,0:T(8,128)(2,1)S(1)} all-to-all(bf16[32,24,128]{2,1,0:T(8,128)(2,1)S(1)} %broadcast_in_dim.8), channel_id=1, replica_groups={{0,16,32,48,64,80,96,112,128,144,160,176,192,208,224,240,256,272,288,30..., dimensions={0} | all-to-all | bytes 393216 | tf_op jit(solution)/shard_map/all_to_all | solution.py:346
  113.0 10.6 %all_to_all.28 = bf16[16,24,128]{2,1,0:T(8,128)(2,1)S(1)} all-to-all(bf16[16,24,128]{2,1,0:T(8,128)(2,1)S(1)} %broadcast_in_dim.9), channel_id=1, replica_groups={{0,1,2,3,4,5,6,7,8,9,10,11,12,13,14,15},{16,17,18,19,20,21,22,23,24,25,..., dimensions={0} | all-to-all | bytes 196608 | tf_op jit(solution)/shard_map/all_to_all | solution.py:346
  123.6 0.8 mirror.1
  (6 shorter events, 0.1 us)
Async XLA Ops:
  0.6 20.7 %copy-start = (bf16[768,256]{1,0:T(8,128)(2,1)S(1)}, bf16[768,256]{1,0:T(8,128)(2,1)}, u32[]{:S(2)}) copy-start(bf16[768,256]{1,0:T(8,128)(2,1)} %param.17) | copy-start | bytes 1179652
  6.5 14.9 %copy-start.2 = (s32[128]{0:T(128)S(1)}, s32[128]{0:T(128)}, u32[]{:S(2)}) copy-start(s32[128]{0:T(128)} %param.16) | copy-start | bytes 1540
  6.5 48.5 %all-to-all-start = ((bf16[64,80,128]{2,1,0:T(8,128)(2,1)}), bf16[64,80,128]{2,1,0:T(8,128)(2,1)S(1)}, u32[]{:S(2)}, u32[]{:S(2)}) async-start(bf16[64,80,128]{2,1,0:T(8,128)(2,1)} %pack_faces.1), calls=%async_computation | async-start | bytes 2621440 | tf_op jit(solution)/shard_map/all_to_all | solution.py:346
  54.9 25.8 %copy-start.1 = (bf16[12,192,128]{2,1,0:T(8,128)(2,1)S(1)}, bf16[12,192,128]{2,1,0:T(8,128)(2,1)}, u32[]{:S(2)}) copy-start(bf16[12,192,128]{2,1,0:T(8,128)(2,1)} %basis_ref.1) | copy-start | bytes 1769476

commit v5 on v4

--- a/solution.py
+++ b/solution.py
@@ -135,7 +135,7 @@
         in_specs=[pl.BlockSpec(memory_space=pl.ANY)] * 6,
         out_specs=pl.BlockSpec(memory_space=pltpu.VMEM),
         scratch_shapes=[
-            pltpu.VMEM((5 * Q * (pairs + 1), LANES), f32),
+            pltpu.VMEM(((5 * Q + 1) * (pairs + 1), LANES), f32),
             pltpu.VMEM(coupling.shape, bf16),
             pltpu.VMEM(factors.shape, bf16),
             pltpu.VMEM(face_diag.shape, f32),
@@ -222,7 +222,7 @@
             pl.BlockSpec(memory_space=pltpu.VMEM),
         ],
         out_specs=pl.BlockSpec(memory_space=pltpu.VMEM),
-        scratch_shapes=[pltpu.VMEM((peers * 33, LANES), f32)],
+        scratch_shapes=[pltpu.VMEM(((peers + 1) * 33, LANES), f32)],
         out_shape=jax.ShapeDtypeStruct((peers, 32, LANES), bf16),
         compiler_params=pltpu.CompilerParams(vmem_limit_bytes=VMEM_LIMIT),
         name="merge_rows",
@@ -309,7 +309,7 @@
         in_specs=[vmem] * 3,
         out_specs=[pl.BlockSpec(memory_space=pltpu.HBM), vmem],
         scratch_shapes=[
-            pltpu.VMEM((Q * (z.shape[1] + 1), LANES), f32),
+            pltpu.VMEM(((Q + 1) * (z.shape[1] + 1), LANES), f32),
             pltpu.VMEM((slots, width, coarse), bf16),
             pltpu.VMEM((slots, width, width), bf16),
             pltpu.SemaphoreType.DMA((slots,)),
@@ -348,6 +348,10 @@
     )
 
 
+def total(x):
+    return lax.optimization_barrier(jnp.sum(x.astype(f32), axis=0)).astype(bf16)
+
+
 def sum_over_all(x, axes):
     peers, groups = (lax.axis_size(a) for a in axes[::-1])
     near = 16
@@ -358,9 +362,9 @@
     far = peers * groups // near
     rows = x.shape[0] // near
     x = x.reshape(near, rows, LANES).astype(bf16)
-    x = jnp.sum(exchange(x, "sub", near_members).astype(f32), axis=0).astype(bf16)
+    x = total(exchange(x, "sub", near_members))
     x = exchange(jnp.broadcast_to(x, (far, rows, LANES)), axes, far_members)
-    x = jnp.sum(x.astype(f32), axis=0).astype(bf16)
+    x = total(x)
     x = exchange(jnp.broadcast_to(x, (near, rows, LANES)), "sub", near_members)
     return x.reshape(near * rows, LANES).astype(f32)
 

time: 125 us -> 125 us (level)
  no operation moved by 1% of the time
where the time goes in v5:
time: 125 us; the launch traced here: 124 us
  blocking collectives  64 us (51%)
  waiting for transfers between devices  33.2 us (27%)
  starting transfers between devices  14.8 us (12%)
  Pallas kernels  11.1 us (9%)
    all_to_all x4, blocking collectives, exchange(): lax.all_to_all(x, axis, split_axis=0, concat_axis=0, tiled=True, axis_ind...  64 us
    all_to_all x1, waiting for transfers between devices, exchange(): lax.all_to_all(x, axis, split_axis=0, concat_axis=0, tiled=True, axis_ind...  33.2 us
    all_to_all x1, starting transfers between devices, exchange(): lax.all_to_all(x, axis, split_axis=0, concat_axis=0, tiled=True, axis_ind...  14.8 us
    pallas_call x1, Pallas kernels, pack_faces(): pl.pallas_call(schur_kernel, in_specs=[pl.BlockSpec(memory_space=pl.ANY)]...  5.81 us
    pallas_call x1, Pallas kernels, owned_and_top(): pl.pallas_call(coarse_kernel, in_specs=[vmem] * 3, out_specs=[pl.BlockSpe...  2.57 us
  transfers between devices with their start and end apart: 1, of which 1 were waited for; matrix products, arithmetic and copies ran while one was open for 0% of the time, Pallas kernels for 0%

profile of v5, /device:TPU:1, one launch (start us, length us, event | category | flops | bytes accessed | tf_op | source)
XLA Modules:
  0.0 124.4 jit_solution(9987568583130066264)
XLA Ops:
  0.6 0.0 copy-start
  0.6 5.8 %pack_faces.1 = bf16[64,80,128]{2,1,0:T(8,128)(2,1)} custom-call(s32[32]{0:T(128)} %block_hbm.1, s32[32]{0:T(128)} %bitcast.10, s32[32]{0:T(128)} %slot_hbm.1, bf16[32,192,192]{2,1,0:T(8,128)(2,1)} %coupling_hbm.1, bf16[4,192,192]{2,1,0:T(8,128)(2,1)} %factors_hbm.1, f32[32,192]{1,0:T(8,128)} %diag_hbm.1), custom_call_target="tpu_custom_call" | custom-call | tf_op jit(solution)/shard_map/pack_faces/pallas_call | solution.py:133
  6.5 0.0 copy-start.2
  6.5 14.8 %all-to-all-start = ((bf16[64,80,128]{2,1,0:T(8,128)(2,1)}), bf16[64,80,128]{2,1,0:T(8,128)(2,1)S(1)}, u32[]{:S(2)}, u32[]{:S(2)}) async-start(bf16[64,80,128]{2,1,0:T(8,128)(2,1)} %pack_faces.1), calls=%async_computation | async-start | bytes 2621440 | tf_op jit(solution)/shard_map/all_to_all | solution.py:346
  21.3 0.0 copy-done
  21.3 0.0 copy-done.2
  21.4 0.4 fusion.rows_ref
  21.7 33.2 %all-to-all-done.x_ref = bf16[64,80,128]{2,1,0:T(8,128)(2,1)S(1)} async-done(((bf16[64,80,128]{2,1,0:T(8,128)(2,1)}), bf16[64,80,128]{2,1,0:T(8,128)(2,1)S(1)}, u32[]{:S(2)}, u32[]{:S(2)}) %all-to-all-start) | async-done | bytes 1310752 | tf_op jit(solution)/shard_map/all_to_all | solution.py:346
  54.9 0.0 copy-start.1
  54.9 2.0 %merge_rows.1 = bf16[64,32,128]{2,1,0:T(8,128)(2,1)S(1)} custom-call(s32[1]{0:T(128)} %bitcast.me_ref, bf16[64,80,128]{2,1,0:T(8,128)(2,1)S(1)} %all-to-all-done.x_ref), custom_call_target="tpu_custom_call" | custom-call | tf_op jit(solution)/shard_map/merge_rows/pallas_call | solution.py:218
  56.9 23.8 %all_to_all.25.z_ref = bf16[64,32,128]{2,1,0:T(8,128)(2,1)S(1)} all-to-all(bf16[64,32,128]{2,1,0:T(8,128)(2,1)S(1)} %merge_rows.1), channel_id=1, replica_groups=mesh['grp'=8,'sub'=64] {'sub'}, dimensions={0} | all-to-all | bytes 1048576 | tf_op jit(solution)/shard_map/all_to_all | solution.py:346
  80.8 0.0 copy-done.1
  80.8 2.6 %owned_and_top.1 = (bf16[12,192,192]{2,1,0:T(8,128)(2,1)}, f32[384,128]{1,0:T(8,128)S(1)}) custom-call(bf16[64,32,128]{2,1,0:T(8,128)(2,1)S(1)} %all_to_all.25.z_ref, bf16[12,192,128]{2,1,0:T(8,128)(2,1)S(1)} %copy-done.1, bf16[256,128]{1,0:T(8,128)(2,1)S(1)} %fusion.rows_ref), custom_call_target="tpu_custom_call" | custom-call | tf_op jit(solution)/shard_map/owned_and_top/pallas_call | solution.py:307
  83.4 10.4 %all_to_all.26 = bf16[16,24,128]{2,1,0:T(8,128)(2,1)S(1)} all-to-all(bf16[16,24,128]{2,1,0:T(8,128)(2,1)S(1)} %bitcast.9), channel_id=1, replica_groups={{0,1,2,3,4,5,6,7,8,9,10,11,12,13,14,15},{16,17,18,19,20,21,22,23,24,25,..., dimensions={0} | all-to-all | bytes 196608 | tf_op jit(solution)/shard_map/all_to_all | solution.py:346
  93.8 19.1 %all_to_all.27 = bf16[32,24,128]{2,1,0:T(8,128)(2,1)S(1)} all-to-all(bf16[32,24,128]{2,1,0:T(8,128)(2,1)S(1)} %broadcast_in_dim.8), channel_id=1, replica_groups={{0,16,32,48,64,80,96,112,128,144,160,176,192,208,224,240,256,272,288,30..., dimensions={0} | all-to-all | bytes 393216 | tf_op jit(solution)/shard_map/all_to_all | solution.py:346
  113.0 10.6 %all_to_all.28 = bf16[16,24,128]{2,1,0:T(8,128)(2,1)S(1)} all-to-all(bf16[16,24,128]{2,1,0:T(8,128)(2,1)S(1)} %broadcast_in_dim.9), channel_id=1, replica_groups={{0,1,2,3,4,5,6,7,8,9,10,11,12,13,14,15},{16,17,18,19,20,21,22,23,24,25,..., dimensions={0} | all-to-all | bytes 196608 | tf_op jit(solution)/shard_map/all_to_all | solution.py:346
  123.6 0.8 mirror.1
  (6 shorter events, 0.1 us)
Async XLA Ops:
  0.6 20.7 %copy-start = (bf16[768,256]{1,0:T(8,128)(2,1)S(1)}, bf16[768,256]{1,0:T(8,128)(2,1)}, u32[]{:S(2)}) copy-start(bf16[768,256]{1,0:T(8,128)(2,1)} %param.17) | copy-start | bytes 1179652
  6.5 14.9 %copy-start.2 = (s32[128]{0:T(128)S(1)}, s32[128]{0:T(128)}, u32[]{:S(2)}) copy-start(s32[128]{0:T(128)} %param.16) | copy-start | bytes 1540
  6.5 48.5 %all-to-all-start = ((bf16[64,80,128]{2,1,0:T(8,128)(2,1)}), bf16[64,80,128]{2,1,0:T(8,128)(2,1)S(1)}, u32[]{:S(2)}, u32[]{:S(2)}) async-start(bf16[64,80,128]{2,1,0:T(8,128)(2,1)} %pack_faces.1), calls=%async_computation | async-start | bytes 2621440 | tf_op jit(solution)/shard_map/all_to_all | solution.py:346
  54.9 25.8 %copy-start.1 = (bf16[12,192,128]{2,1,0:T(8,128)(2,1)S(1)}, bf16[12,192,128]{2,1,0:T(8,128)(2,1)}, u32[]{:S(2)}) copy-start(bf16[12,192,128]{2,1,0:T(8,128)(2,1)} %basis_ref.1) | copy-start | bytes 1769476

commit v6 on v5

--- a/solution.py
+++ b/solution.py
@@ -62,13 +62,13 @@
         pltpu.make_async_copy(owner_hbm, owner_ref, sems.at[3 + steps]),
         pltpu.make_async_copy(slot_hbm, slot_ref, sems.at[4 + steps]),
     ]
-    for copy in copies:
+    for copy in copies[:2] + copies[-3:] + copies[2:-3]:
         copy.start()
     left, d, keep = masks()
     eye = d == 0
     eye_right = eye & ~left
-    copies[0].wait()
-    copies[1].wait()
+    for copy in copies[:2] + copies[-3:]:
+        copy.wait()
     for s in range(steps):
         copies[2 + s].wait()
         interiors = []
@@ -85,9 +85,6 @@
             lax.dot_general(x, x, (((0,), (0,)), ((), ())), preferred_element_type=f32)
             for x in interiors
         ]
-        if s == 0:
-            for copy in copies[-3:]:
-                copy.wait()
         last = None
         for q, g in enumerate(grams):
             face = s * STEP_FACES + q
@@ -247,6 +244,10 @@
     eye = d == 0
     for j in range(Q):
         flat[step * j : step * j + rows, :] = z_ref[j].astype(f32)
+    copies = [
+        pltpu.make_async_copy(owned_ref.at[r], owned_hbm.at[r], sems.at[r])
+        for r in range(slots)
+    ]
     for q in range(half):
         f_both = flat[pl.ds(slots * 2 + q, Q, stride=step), :]
         f_turned = f_both.T
@@ -269,12 +270,7 @@
             owned_ref[r, Q : 2 * Q, LANES:] = t1[:, :Q].astype(bf16)
             owned_ref[r, 2 * Q :, :LANES] = turned[:Q].astype(bf16)
             owned_ref[r, 2 * Q :, LANES:] = d3.astype(bf16)
-    copies = [
-        pltpu.make_async_copy(owned_ref.at[r], owned_hbm.at[r], sems.at[r])
-        for r in range(slots)
-    ]
-    for copy in copies:
-        copy.start()
+            copies[r].start()
     for r in range(slots):
         applied[r] = jnp.dot(
             owned_ref[r], basis_ref[r], preferred_element_type=f32
@@ -348,25 +344,19 @@
     )
 
 
-def total(x):
-    return lax.optimization_barrier(jnp.sum(x.astype(f32), axis=0)).astype(bf16)
-
-
 def sum_over_all(x, axes):
     peers, groups = (lax.axis_size(a) for a in axes[::-1])
     near = 16
-    near_members = [[k * near + i for i in range(near)] for k in range(peers // near)]
-    far_members = [
-        list(range(i, peers * groups, near)) for i in range(near)
-    ]
     far = peers * groups // near
     rows = x.shape[0] // near
-    x = x.reshape(near, rows, LANES).astype(bf16)
-    x = total(exchange(x, "sub", near_members))
+    near_members = [[k * near + i for i in range(near)] for k in range(peers // near)]
+    far_members = [list(range(i, peers * groups, near)) for i in range(near)]
+    x = exchange(x.astype(bf16).reshape(near, rows, LANES), axes[1], near_members)
+    x = jnp.sum(x.astype(f32), axis=0).astype(bf16)
     x = exchange(jnp.broadcast_to(x, (far, rows, LANES)), axes, far_members)
-    x = total(x)
-    x = exchange(jnp.broadcast_to(x, (near, rows, LANES)), "sub", near_members)
-    return x.reshape(near * rows, LANES).astype(f32)
+    x = jnp.sum(x.astype(f32), axis=0)
+    x = exchange(jnp.broadcast_to(x, (near, rows, LANES)), axes[1], near_members)
+    return x.reshape(near * rows, LANES)
 
 
 def local(

time: 125 us -> 125 us (level)
  no operation moved by 1% of the time
where the time goes in v6:
time: 125 us; the launch traced here: 124 us
  blocking collectives  64.8 us (52%)
  waiting for transfers between devices  33.2 us (27%)
  starting transfers between devices  14.8 us (12%)
  Pallas kernels  10.2 us (8%)
    all_to_all x4, blocking collectives, exchange(): lax.all_to_all(x, axis, split_axis=0, concat_axis=0, tiled=True, axis_ind...  64.8 us
    all_to_all x1, waiting for transfers between devices, exchange(): lax.all_to_all(x, axis, split_axis=0, concat_axis=0, tiled=True, axis_ind...  33.2 us
    all_to_all x1, starting transfers between devices, exchange(): lax.all_to_all(x, axis, split_axis=0, concat_axis=0, tiled=True, axis_ind...  14.8 us
    pallas_call x1, Pallas kernels, pack_faces(): pl.pallas_call(schur_kernel, in_specs=[pl.BlockSpec(memory_space=pl.ANY)]...  5.59 us
  transfers between devices with their start and end apart: 1, of which 1 were waited for; matrix products, arithmetic and copies ran while one was open for 0% of the time, Pallas kernels for 0%

profile of v6, /device:TPU:1, one launch (start us, length us, event | category | flops | bytes accessed | tf_op | source)
XLA Modules:
  0.0 124.3 jit_solution(17264691931141797764)
XLA Ops:
  0.6 0.0 copy-start
  0.6 5.6 %pack_faces.1 = bf16[64,80,128]{2,1,0:T(8,128)(2,1)} custom-call(s32[32]{0:T(128)} %block_hbm.1, s32[32]{0:T(128)} %bitcast.9, s32[32]{0:T(128)} %slot_hbm.1, bf16[32,192,192]{2,1,0:T(8,128)(2,1)} %coupling_hbm.1, bf16[4,192,192]{2,1,0:T(8,128)(2,1)} %factors_hbm.1, f32[32,192]{1,0:T(8,128)} %diag_hbm.1), custom_call_target="tpu_custom_call" | custom-call | tf_op jit(solution)/shard_map/pack_faces/pallas_call | solution.py:130
  6.2 0.0 copy-start.2
  6.3 14.8 %all-to-all-start = ((bf16[64,80,128]{2,1,0:T(8,128)(2,1)}), bf16[64,80,128]{2,1,0:T(8,128)(2,1)S(1)}, u32[]{:S(2)}, u32[]{:S(2)}) async-start(bf16[64,80,128]{2,1,0:T(8,128)(2,1)} %pack_faces.1), calls=%async_computation | async-start | bytes 2621440 | tf_op jit(solution)/shard_map/all_to_all | solution.py:342
  21.1 0.0 copy-done
  21.1 0.0 copy-done.2
  21.1 0.4 fusion.rows_ref
  21.5 33.2 %all-to-all-done.x_ref = bf16[64,80,128]{2,1,0:T(8,128)(2,1)S(1)} async-done(((bf16[64,80,128]{2,1,0:T(8,128)(2,1)}), bf16[64,80,128]{2,1,0:T(8,128)(2,1)S(1)}, u32[]{:S(2)}, u32[]{:S(2)}) %all-to-all-start) | async-done | bytes 1310752 | tf_op jit(solution)/shard_map/all_to_all | solution.py:342
  54.7 0.0 copy-start.1
  54.7 2.0 %merge_rows.1 = bf16[64,32,128]{2,1,0:T(8,128)(2,1)S(1)} custom-call(s32[1]{0:T(128)} %bitcast.me_ref, bf16[64,80,128]{2,1,0:T(8,128)(2,1)S(1)} %all-to-all-done.x_ref), custom_call_target="tpu_custom_call" | custom-call | tf_op jit(solution)/shard_map/merge_rows/pallas_call | solution.py:215
  56.7 23.8 %all_to_all.25.z_ref = bf16[64,32,128]{2,1,0:T(8,128)(2,1)S(1)} all-to-all(bf16[64,32,128]{2,1,0:T(8,128)(2,1)S(1)} %merge_rows.1), channel_id=1, replica_groups=mesh['grp'=8,'sub'=64] {'sub'}, dimensions={0} | all-to-all | bytes 1048576 | tf_op jit(solution)/shard_map/all_to_all | solution.py:342
  80.5 0.0 copy-done.1
  80.5 1.8 %owned_and_top.1 = (bf16[12,192,192]{2,1,0:T(8,128)(2,1)}, f32[384,128]{1,0:T(8,128)S(1)}) custom-call(bf16[64,32,128]{2,1,0:T(8,128)(2,1)S(1)} %all_to_all.25.z_ref, bf16[12,192,128]{2,1,0:T(8,128)(2,1)S(1)} %copy-done.1, bf16[256,128]{1,0:T(8,128)(2,1)S(1)} %fusion.rows_ref), custom_call_target="tpu_custom_call" | custom-call | tf_op jit(solution)/shard_map/owned_and_top/pallas_call | solution.py:303
  82.4 10.4 %all_to_all.26 = bf16[16,24,128]{2,1,0:T(8,128)(2,1)S(1)} all-to-all(bf16[16,24,128]{2,1,0:T(8,128)(2,1)S(1)} %bitcast.8), channel_id=1, replica_groups={{0,1,2,3,4,5,6,7,8,9,10,11,12,13,14,15},{16,17,18,19,20,21,22,23,24,25,..., dimensions={0} | all-to-all | bytes 196608 | tf_op jit(solution)/shard_map/all_to_all | solution.py:342
  92.8 19.1 %all_to_all.27 = bf16[32,24,128]{2,1,0:T(8,128)(2,1)S(1)} all-to-all(bf16[32,24,128]{2,1,0:T(8,128)(2,1)S(1)} %broadcast_in_dim.8), channel_id=1, replica_groups={{0,16,32,48,64,80,96,112,128,144,160,176,192,208,224,240,256,272,288,30..., dimensions={0} | all-to-all | bytes 393216 | tf_op jit(solution)/shard_map/all_to_all | solution.py:342
  112.0 11.5 %all_to_all.28 = f32[16,24,128]{2,1,0:T(8,128)S(1)} all-to-all(f32[16,24,128]{2,1,0:T(8,128)S(1)} %broadcast_in_dim.9), channel_id=1, replica_groups={{0,1,2,3,4,5,6,7,8,9,10,11,12,13,14,15},{16,17,18,19,20,21,22,23,24,25,..., dimensions={0} | all-to-all | bytes 393216 | tf_op jit(solution)/shard_map/all_to_all | solution.py:342
  123.5 0.8 mirror.1
  (5 shorter events, 0.1 us)
Async XLA Ops:
  0.6 20.5 %copy-start = (bf16[768,256]{1,0:T(8,128)(2,1)S(1)}, bf16[768,256]{1,0:T(8,128)(2,1)}, u32[]{:S(2)}) copy-start(bf16[768,256]{1,0:T(8,128)(2,1)} %param.17) | copy-start | bytes 1179652
  6.2 14.9 %copy-start.2 = (s32[128]{0:T(128)S(1)}, s32[128]{0:T(128)}, u32[]{:S(2)}) copy-start(s32[128]{0:T(128)} %param.16) | copy-start | bytes 1540
  6.3 48.5 %all-to-all-start = ((bf16[64,80,128]{2,1,0:T(8,128)(2,1)}), bf16[64,80,128]{2,1,0:T(8,128)(2,1)S(1)}, u32[]{:S(2)}, u32[]{:S(2)}) async-start(bf16[64,80,128]{2,1,0:T(8,128)(2,1)} %pack_faces.1), calls=%async_computation | async-start | bytes 2621440 | tf_op jit(solution)/shard_map/all_to_all | solution.py:342
  54.7 25.8 %copy-start.1 = (bf16[12,192,128]{2,1,0:T(8,128)(2,1)S(1)}, bf16[12,192,128]{2,1,0:T(8,128)(2,1)}, u32[]{:S(2)}) copy-start(bf16[12,192,128]{2,1,0:T(8,128)(2,1)} %basis_ref.1) | copy-start | bytes 1769476

commit v7 on v6

--- a/solution.py
+++ b/solution.py
@@ -7,7 +7,7 @@
 
 Q = 64
 LANES = 128
-STEP_FACES = 16
+CUTS = (0, 8, 32)
 KEEP, OWNER_AT, SLOT_AT = 63, 61, 60
 PACK_VMEM = 56 * 1024 * 1024
 VMEM_LIMIT = 16 * 1024 * 1024
@@ -44,14 +44,14 @@
     sems,
 ):
     faces = coupling_ref.shape[0]
-    steps = faces // STEP_FACES
+    steps = len(CUTS) - 1
     pairs = faces // 2
     copies = [
         pltpu.make_async_copy(block_hbm, block_ref, sems.at[0]),
         pltpu.make_async_copy(factors_hbm, factors_ref, sems.at[1]),
     ]
     for s in range(steps):
-        part = pl.ds(s * STEP_FACES, STEP_FACES)
+        part = pl.ds(CUTS[s], CUTS[s + 1] - CUTS[s])
         copies.append(
             pltpu.make_async_copy(
                 coupling_hbm.at[part], coupling_ref.at[part], sems.at[2 + s]
@@ -72,7 +72,7 @@
     for s in range(steps):
         copies[2 + s].wait()
         interiors = []
-        for face in range(s * STEP_FACES, (s + 1) * STEP_FACES):
+        for face in range(CUTS[s], CUTS[s + 1]):
             c = coupling_ref[face]
             mid = c[:, Q : 2 * Q]
             columns = jnp.concatenate([c[:, 2 * Q :], mid, mid, c[:, :Q]], axis=1)
@@ -87,7 +87,7 @@
         ]
         last = None
         for q, g in enumerate(grams):
-            face = s * STEP_FACES + q
+            face = CUTS[s] + q
             d3, r1 = g[:Q, :LANES], g[Q : 2 * Q, :LANES]
             t0, d1 = g[3 * Q :, :LANES], g[3 * Q :, LANES:]
             diag01 = diag_ref[face : face + 1, :LANES]
@@ -139,7 +139,7 @@
             pltpu.SMEM((faces,), i32),
             pltpu.SMEM((faces,), i32),
             pltpu.SMEM((faces,), i32),
-            pltpu.SemaphoreType.DMA((5 + faces // STEP_FACES,)),
+            pltpu.SemaphoreType.DMA((4 + len(CUTS),)),
         ],
         out_shape=jax.ShapeDtypeStruct((Q, 5 * pairs, LANES), bf16),
         compiler_params=pltpu.CompilerParams(vmem_limit_bytes=PACK_VMEM),

time: 125 us -> 124 us (level)
  no operation moved by 1% of the time
where the time goes in v7:
time: 124 us
  blocking collectives  64.8 us (52%)
  waiting for transfers between devices  33.2 us (27%)
  starting transfers between devices  14.8 us (12%)
  Pallas kernels  10 us (8%)
    all_to_all x4, blocking collectives, exchange(): lax.all_to_all(x, axis, split_axis=0, concat_axis=0, tiled=True, axis_ind...  64.8 us
    all_to_all x1, waiting for transfers between devices, exchange(): lax.all_to_all(x, axis, split_axis=0, concat_axis=0, tiled=True, axis_ind...  33.2 us
    all_to_all x1, starting transfers between devices, exchange(): lax.all_to_all(x, axis, split_axis=0, concat_axis=0, tiled=True, axis_ind...  14.8 us
    pallas_call x1, Pallas kernels, pack_faces(): pl.pallas_call(schur_kernel, in_specs=[pl.BlockSpec(memory_space=pl.ANY)]...  5.42 us
  transfers between devices with their start and end apart: 1, of which 1 were waited for; matrix products, arithmetic and copies ran while one was open for 0% of the time, Pallas kernels for 0%

profile of v7, /device:TPU:1, one launch (start us, length us, event | category | flops | bytes accessed | tf_op | source)
XLA Modules:
  0.0 124.1 jit_solution(607159600931208696)
XLA Ops:
  0.6 0.0 copy-start
  0.6 5.4 %pack_faces.1 = bf16[64,80,128]{2,1,0:T(8,128)(2,1)} custom-call(s32[32]{0:T(128)} %block_hbm.1, s32[32]{0:T(128)} %bitcast.9, s32[32]{0:T(128)} %slot_hbm.1, bf16[32,192,192]{2,1,0:T(8,128)(2,1)} %coupling_hbm.1, bf16[4,192,192]{2,1,0:T(8,128)(2,1)} %factors_hbm.1, f32[32,192]{1,0:T(8,128)} %diag_hbm.1), custom_call_target="tpu_custom_call" | custom-call | tf_op jit(solution)/shard_map/pack_faces/pallas_call | solution.py:130
  6.1 0.0 copy-start.2
  6.1 14.8 %all-to-all-start = ((bf16[64,80,128]{2,1,0:T(8,128)(2,1)}), bf16[64,80,128]{2,1,0:T(8,128)(2,1)S(1)}, u32[]{:S(2)}, u32[]{:S(2)}) async-start(bf16[64,80,128]{2,1,0:T(8,128)(2,1)} %pack_faces.1), calls=%async_computation | async-start | bytes 2621440 | tf_op jit(solution)/shard_map/all_to_all | solution.py:342
  20.9 0.0 copy-done
  21.0 0.0 copy-done.2
  21.0 0.4 fusion.rows_ref
  21.3 33.2 %all-to-all-done.x_ref = bf16[64,80,128]{2,1,0:T(8,128)(2,1)S(1)} async-done(((bf16[64,80,128]{2,1,0:T(8,128)(2,1)}), bf16[64,80,128]{2,1,0:T(8,128)(2,1)S(1)}, u32[]{:S(2)}, u32[]{:S(2)}) %all-to-all-start) | async-done | bytes 1310752 | tf_op jit(solution)/shard_map/all_to_all | solution.py:342
  54.5 0.0 copy-start.1
  54.5 2.0 %merge_rows.1 = bf16[64,32,128]{2,1,0:T(8,128)(2,1)S(1)} custom-call(s32[1]{0:T(128)} %bitcast.me_ref, bf16[64,80,128]{2,1,0:T(8,128)(2,1)S(1)} %all-to-all-done.x_ref), custom_call_target="tpu_custom_call" | custom-call | tf_op jit(solution)/shard_map/merge_rows/pallas_call | solution.py:215
  56.5 23.8 %all_to_all.25.z_ref = bf16[64,32,128]{2,1,0:T(8,128)(2,1)S(1)} all-to-all(bf16[64,32,128]{2,1,0:T(8,128)(2,1)S(1)} %merge_rows.1), channel_id=1, replica_groups=mesh['grp'=8,'sub'=64] {'sub'}, dimensions={0} | all-to-all | bytes 1048576 | tf_op jit(solution)/shard_map/all_to_all | solution.py:342
  80.4 0.0 copy-done.1
  80.4 1.8 %owned_and_top.1 = (bf16[12,192,192]{2,1,0:T(8,128)(2,1)}, f32[384,128]{1,0:T(8,128)S(1)}) custom-call(bf16[64,32,128]{2,1,0:T(8,128)(2,1)S(1)} %all_to_all.25.z_ref, bf16[12,192,128]{2,1,0:T(8,128)(2,1)S(1)} %copy-done.1, bf16[256,128]{1,0:T(8,128)(2,1)S(1)} %fusion.rows_ref), custom_call_target="tpu_custom_call" | custom-call | tf_op jit(solution)/shard_map/owned_and_top/pallas_call | solution.py:303
  82.2 10.4 %all_to_all.26 = bf16[16,24,128]{2,1,0:T(8,128)(2,1)S(1)} all-to-all(bf16[16,24,128]{2,1,0:T(8,128)(2,1)S(1)} %bitcast.8), channel_id=1, replica_groups={{0,1,2,3,4,5,6,7,8,9,10,11,12,13,14,15},{16,17,18,19,20,21,22,23,24,25,..., dimensions={0} | all-to-all | bytes 196608 | tf_op jit(solution)/shard_map/all_to_all | solution.py:342
  92.7 19.1 %all_to_all.27 = bf16[32,24,128]{2,1,0:T(8,128)(2,1)S(1)} all-to-all(bf16[32,24,128]{2,1,0:T(8,128)(2,1)S(1)} %broadcast_in_dim.8), channel_id=1, replica_groups={{0,16,32,48,64,80,96,112,128,144,160,176,192,208,224,240,256,272,288,30..., dimensions={0} | all-to-all | bytes 393216 | tf_op jit(solution)/shard_map/all_to_all | solution.py:342
  111.8 11.5 %all_to_all.28 = f32[16,24,128]{2,1,0:T(8,128)S(1)} all-to-all(f32[16,24,128]{2,1,0:T(8,128)S(1)} %broadcast_in_dim.9), channel_id=1, replica_groups={{0,1,2,3,4,5,6,7,8,9,10,11,12,13,14,15},{16,17,18,19,20,21,22,23,24,25,..., dimensions={0} | all-to-all | bytes 393216 | tf_op jit(solution)/shard_map/all_to_all | solution.py:342
  123.3 0.8 mirror.1
  (5 shorter events, 0.1 us)
Async XLA Ops:
  0.6 20.3 %copy-start = (bf16[768,256]{1,0:T(8,128)(2,1)S(1)}, bf16[768,256]{1,0:T(8,128)(2,1)}, u32[]{:S(2)}) copy-start(bf16[768,256]{1,0:T(8,128)(2,1)} %param.17) | copy-start | bytes 1179652
  6.1 14.9 %copy-start.2 = (s32[128]{0:T(128)S(1)}, s32[128]{0:T(128)}, u32[]{:S(2)}) copy-start(s32[128]{0:T(128)} %param.16) | copy-start | bytes 1540
  6.1 48.5 %all-to-all-start = ((bf16[64,80,128]{2,1,0:T(8,128)(2,1)}), bf16[64,80,128]{2,1,0:T(8,128)(2,1)S(1)}, u32[]{:S(2)}, u32[]{:S(2)}) async-start(bf16[64,80,128]{2,1,0:T(8,128)(2,1)} %pack_faces.1), calls=%async_computation | async-start | bytes 2621440 | tf_op jit(solution)/shard_map/all_to_all | solution.py:342
  54.5 25.8 %copy-start.1 = (bf16[12,192,128]{2,1,0:T(8,128)(2,1)S(1)}, bf16[12,192,128]{2,1,0:T(8,128)(2,1)}, u32[]{:S(2)}) copy-start(bf16[12,192,128]{2,1,0:T(8,128)(2,1)} %basis_ref.1) | copy-start | bytes 1769476

commit v8 on v7

--- a/solution.py
+++ b/solution.py
@@ -346,16 +346,21 @@
 
 def sum_over_all(x, axes):
     peers, groups = (lax.axis_size(a) for a in axes[::-1])
-    near = 16
+    pn, gn = 8, 2
+    near = pn * gn
     far = peers * groups // near
     rows = x.shape[0] // near
-    near_members = [[k * near + i for i in range(near)] for k in range(peers // near)]
-    far_members = [list(range(i, peers * groups, near)) for i in range(near)]
-    x = exchange(x.astype(bf16).reshape(near, rows, LANES), axes[1], near_members)
+    near_members = [
+        [(g * gn + i) * peers + p * pn + j for i in range(gn) for j in range(pn)]
+        for g in range(groups // gn)
+        for p in range(peers // pn)
+    ]
+    far_members = [list(m) for m in zip(*near_members)]
+    x = exchange(x.astype(bf16).reshape(near, rows, LANES), axes, near_members)
     x = jnp.sum(x.astype(f32), axis=0).astype(bf16)
     x = exchange(jnp.broadcast_to(x, (far, rows, LANES)), axes, far_members)
     x = jnp.sum(x.astype(f32), axis=0)
-    x = exchange(jnp.broadcast_to(x, (near, rows, LANES)), axes[1], near_members)
+    x = exchange(jnp.broadcast_to(x, (near, rows, LANES)), axes, near_members)
     return x.reshape(near * rows, LANES)
 
 

time: 124 us -> 125 us (level)
  no operation moved by 1% of the time
where the time goes in v8:
time: 125 us; the launch traced here: 124 us
  blocking collectives  65 us (52%)
  waiting for transfers between devices  33.2 us (27%)
  starting transfers between devices  14.8 us (12%)
  Pallas kernels  10 us (8%)
    all_to_all x4, blocking collectives, exchange(): lax.all_to_all(x, axis, split_axis=0, concat_axis=0, tiled=True, axis_ind...  65 us
    all_to_all x1, waiting for transfers between devices, exchange(): lax.all_to_all(x, axis, split_axis=0, concat_axis=0, tiled=True, axis_ind...  33.2 us
    all_to_all x1, starting transfers between devices, exchange(): lax.all_to_all(x, axis, split_axis=0, concat_axis=0, tiled=True, axis_ind...  14.8 us
    pallas_call x1, Pallas kernels, pack_faces(): pl.pallas_call(schur_kernel, in_specs=[pl.BlockSpec(memory_space=pl.ANY)]...  5.42 us
  transfers between devices with their start and end apart: 1, of which 1 were waited for; matrix products, arithmetic and copies ran while one was open for 0% of the time, Pallas kernels for 0%

profile of v8, /device:TPU:1, one launch (start us, length us, event | category | flops | bytes accessed | tf_op | source)
XLA Modules:
  0.0 124.3 jit_solution(1870838429520930439)
XLA Ops:
  0.6 0.0 copy-start
  0.6 5.4 %pack_faces.1 = bf16[64,80,128]{2,1,0:T(8,128)(2,1)} custom-call(s32[32]{0:T(128)} %block_hbm.1, s32[32]{0:T(128)} %bitcast.9, s32[32]{0:T(128)} %slot_hbm.1, bf16[32,192,192]{2,1,0:T(8,128)(2,1)} %coupling_hbm.1, bf16[4,192,192]{2,1,0:T(8,128)(2,1)} %factors_hbm.1, f32[32,192]{1,0:T(8,128)} %diag_hbm.1), custom_call_target="tpu_custom_call" | custom-call | tf_op jit(solution)/shard_map/pack_faces/pallas_call | solution.py:130
  6.1 0.0 copy-start.2
  6.1 14.8 %all-to-all-start = ((bf16[64,80,128]{2,1,0:T(8,128)(2,1)}), bf16[64,80,128]{2,1,0:T(8,128)(2,1)S(1)}, u32[]{:S(2)}, u32[]{:S(2)}) async-start(bf16[64,80,128]{2,1,0:T(8,128)(2,1)} %pack_faces.1), calls=%async_computation | async-start | bytes 2621440 | tf_op jit(solution)/shard_map/all_to_all | solution.py:342
  20.9 0.0 copy-done
  21.0 0.0 copy-done.2
  21.0 0.4 fusion.rows_ref
  21.3 33.2 %all-to-all-done.x_ref = bf16[64,80,128]{2,1,0:T(8,128)(2,1)S(1)} async-done(((bf16[64,80,128]{2,1,0:T(8,128)(2,1)}), bf16[64,80,128]{2,1,0:T(8,128)(2,1)S(1)}, u32[]{:S(2)}, u32[]{:S(2)}) %all-to-all-start) | async-done | bytes 1310752 | tf_op jit(solution)/shard_map/all_to_all | solution.py:342
  54.5 0.0 copy-start.1
  54.5 2.0 %merge_rows.1 = bf16[64,32,128]{2,1,0:T(8,128)(2,1)S(1)} custom-call(s32[1]{0:T(128)} %bitcast.me_ref, bf16[64,80,128]{2,1,0:T(8,128)(2,1)S(1)} %all-to-all-done.x_ref), custom_call_target="tpu_custom_call" | custom-call | tf_op jit(solution)/shard_map/merge_rows/pallas_call | solution.py:215
  56.5 23.8 %all_to_all.25.z_ref = bf16[64,32,128]{2,1,0:T(8,128)(2,1)S(1)} all-to-all(bf16[64,32,128]{2,1,0:T(8,128)(2,1)S(1)} %merge_rows.1), channel_id=1, replica_groups=mesh['grp'=8,'sub'=64] {'sub'}, dimensions={0} | all-to-all | bytes 1048576 | tf_op jit(solution)/shard_map/all_to_all | solution.py:342
  80.4 0.0 copy-done.1
  80.4 1.8 %owned_and_top.1 = (bf16[12,192,192]{2,1,0:T(8,128)(2,1)}, f32[384,128]{1,0:T(8,128)S(1)}) custom-call(bf16[64,32,128]{2,1,0:T(8,128)(2,1)S(1)} %all_to_all.25.z_ref, bf16[12,192,128]{2,1,0:T(8,128)(2,1)S(1)} %copy-done.1, bf16[256,128]{1,0:T(8,128)(2,1)S(1)} %fusion.rows_ref), custom_call_target="tpu_custom_call" | custom-call | tf_op jit(solution)/shard_map/owned_and_top/pallas_call | solution.py:303
  82.2 11.3 %all_to_all.26 = bf16[16,24,128]{2,1,0:T(8,128)(2,1)S(1)} all-to-all(bf16[16,24,128]{2,1,0:T(8,128)(2,1)S(1)} %bitcast.8), channel_id=1, replica_groups={{0,1,2,3,4,5,6,7,64,65,66,67,68,69,70,71},{8,9,10,11,12,13,14,15,72,73,..., dimensions={0} | all-to-all | bytes 196608 | tf_op jit(solution)/shard_map/all_to_all | solution.py:342
  93.6 18.6 %all_to_all.27 = bf16[32,24,128]{2,1,0:T(8,128)(2,1)S(1)} all-to-all(bf16[32,24,128]{2,1,0:T(8,128)(2,1)S(1)} %broadcast_in_dim.8), channel_id=1, replica_groups={{0,8,16,24,32,40,48,56,128,136,144,152,160,168,176,184,256,264,272,280,..., dimensions={0} | all-to-all | bytes 393216 | tf_op jit(solution)/shard_map/all_to_all | solution.py:342
  112.3 11.2 %all_to_all.28 = f32[16,24,128]{2,1,0:T(8,128)S(1)} all-to-all(f32[16,24,128]{2,1,0:T(8,128)S(1)} %broadcast_in_dim.9), channel_id=1, replica_groups={{0,1,2,3,4,5,6,7,64,65,66,67,68,69,70,71},{8,9,10,11,12,13,14,15,72,73,..., dimensions={0} | all-to-all | bytes 393216 | tf_op jit(solution)/shard_map/all_to_all | solution.py:342
  123.5 0.8 mirror.1
  (5 shorter events, 0.1 us)
Async XLA Ops:
  0.6 20.3 %copy-start = (bf16[768,256]{1,0:T(8,128)(2,1)S(1)}, bf16[768,256]{1,0:T(8,128)(2,1)}, u32[]{:S(2)}) copy-start(bf16[768,256]{1,0:T(8,128)(2,1)} %param.17) | copy-start | bytes 1179652
  6.1 14.9 %copy-start.2 = (s32[128]{0:T(128)S(1)}, s32[128]{0:T(128)}, u32[]{:S(2)}) copy-start(s32[128]{0:T(128)} %param.16) | copy-start | bytes 1540
  6.1 48.5 %all-to-all-start = ((bf16[64,80,128]{2,1,0:T(8,128)(2,1)}), bf16[64,80,128]{2,1,0:T(8,128)(2,1)S(1)}, u32[]{:S(2)}, u32[]{:S(2)}) async-start(bf16[64,80,128]{2,1,0:T(8,128)(2,1)} %pack_faces.1), calls=%async_computation | async-start | bytes 2621440 | tf_op jit(solution)/shard_map/all_to_all | solution.py:342
  54.5 25.8 %copy-start.1 = (bf16[12,192,128]{2,1,0:T(8,128)(2,1)S(1)}, bf16[12,192,128]{2,1,0:T(8,128)(2,1)}, u32[]{:S(2)}) copy-start(bf16[12,192,128]{2,1,0:T(8,128)(2,1)} %basis_ref.1) | copy-start | bytes 1769476

commit v9 on v7

--- a/solution.py
+++ b/solution.py
@@ -290,9 +290,9 @@
     for part in split3(inner):
         upper += jnp.dot(rows_t[:LANES], part, preferred_element_type=f32)
         lower += jnp.dot(rows_t[LANES:], part[:, LANES:], preferred_element_type=f32)
-    top_ref[:LANES, :] = upper[:, :LANES]
-    top_ref[LANES : 2 * LANES, :] = upper[:, LANES:]
-    top_ref[2 * LANES :, :] = lower
+    top_ref[:LANES, :] = upper[:, :LANES].astype(bf16)
+    top_ref[LANES : 2 * LANES, :] = upper[:, LANES:].astype(bf16)
+    top_ref[2 * LANES :, :] = lower.astype(bf16)
     for copy in copies:
         copy.wait()
 
@@ -312,7 +312,7 @@
         ],
         out_shape=[
             jax.ShapeDtypeStruct((slots, width, width), bf16),
-            jax.ShapeDtypeStruct((3 * LANES, LANES), f32),
+            jax.ShapeDtypeStruct((3 * LANES, LANES), bf16),
         ],
         compiler_params=pltpu.CompilerParams(vmem_limit_bytes=VMEM_LIMIT),
         name="owned_and_top",
@@ -351,7 +351,7 @@
     rows = x.shape[0] // near
     near_members = [[k * near + i for i in range(near)] for k in range(peers // near)]
     far_members = [list(range(i, peers * groups, near)) for i in range(near)]
-    x = exchange(x.astype(bf16).reshape(near, rows, LANES), axes[1], near_members)
+    x = exchange(x.reshape(near, rows, LANES), axes[1], near_members)
     x = jnp.sum(x.astype(f32), axis=0).astype(bf16)
     x = exchange(jnp.broadcast_to(x, (far, rows, LANES)), axes, far_members)
     x = jnp.sum(x.astype(f32), axis=0)

time: 124 us -> 124 us (level)
  no operation moved by 1% of the time
where the time goes in v9:
time: 124 us
  blocking collectives  64.8 us (52%)
  waiting for transfers between devices  33.2 us (27%)
  starting transfers between devices  14.8 us (12%)
  Pallas kernels  10 us (8%)
    all_to_all x4, blocking collectives, exchange(): lax.all_to_all(x, axis, split_axis=0, concat_axis=0, tiled=True, axis_ind...  64.8 us
    all_to_all x1, waiting for transfers between devices, exchange(): lax.all_to_all(x, axis, split_axis=0, concat_axis=0, tiled=True, axis_ind...  33.2 us
    all_to_all x1, starting transfers between devices, exchange(): lax.all_to_all(x, axis, split_axis=0, concat_axis=0, tiled=True, axis_ind...  14.8 us
    pallas_call x1, Pallas kernels, pack_faces(): pl.pallas_call(schur_kernel, in_specs=[pl.BlockSpec(memory_space=pl.ANY)]...  5.42 us
  transfers between devices with their start and end apart: 1, of which 1 were waited for; matrix products, arithmetic and copies ran while one was open for 0% of the time, Pallas kernels for 0%

profile of v9, /device:TPU:1, one launch (start us, length us, event | category | flops | bytes accessed | tf_op | source)
XLA Modules:
  0.0 124.1 jit_solution(6231717078106994416)
XLA Ops:
  0.6 0.0 copy-start
  0.6 5.4 %pack_faces.1 = bf16[64,80,128]{2,1,0:T(8,128)(2,1)} custom-call(s32[32]{0:T(128)} %block_hbm.1, s32[32]{0:T(128)} %bitcast.9, s32[32]{0:T(128)} %slot_hbm.1, bf16[32,192,192]{2,1,0:T(8,128)(2,1)} %coupling_hbm.1, bf16[4,192,192]{2,1,0:T(8,128)(2,1)} %factors_hbm.1, f32[32,192]{1,0:T(8,128)} %diag_hbm.1), custom_call_target="tpu_custom_call" | custom-call | tf_op jit(solution)/shard_map/pack_faces/pallas_call | solution.py:130
  6.1 0.0 copy-start.2
  6.1 14.8 %all-to-all-start = ((bf16[64,80,128]{2,1,0:T(8,128)(2,1)}), bf16[64,80,128]{2,1,0:T(8,128)(2,1)S(1)}, u32[]{:S(2)}, u32[]{:S(2)}) async-start(bf16[64,80,128]{2,1,0:T(8,128)(2,1)} %pack_faces.1), calls=%async_computation | async-start | bytes 2621440 | tf_op jit(solution)/shard_map/all_to_all | solution.py:342
  20.9 0.0 copy-done
  21.0 0.0 copy-done.2
  21.0 0.4 fusion.rows_ref
  21.3 33.2 %all-to-all-done.x_ref = bf16[64,80,128]{2,1,0:T(8,128)(2,1)S(1)} async-done(((bf16[64,80,128]{2,1,0:T(8,128)(2,1)}), bf16[64,80,128]{2,1,0:T(8,128)(2,1)S(1)}, u32[]{:S(2)}, u32[]{:S(2)}) %all-to-all-start) | async-done | bytes 1310752 | tf_op jit(solution)/shard_map/all_to_all | solution.py:342
  54.5 0.0 copy-start.1
  54.5 2.0 %merge_rows.1 = bf16[64,32,128]{2,1,0:T(8,128)(2,1)S(1)} custom-call(s32[1]{0:T(128)} %bitcast.me_ref, bf16[64,80,128]{2,1,0:T(8,128)(2,1)S(1)} %all-to-all-done.x_ref), custom_call_target="tpu_custom_call" | custom-call | tf_op jit(solution)/shard_map/merge_rows/pallas_call | solution.py:215
  56.5 23.8 %all_to_all.25.z_ref = bf16[64,32,128]{2,1,0:T(8,128)(2,1)S(1)} all-to-all(bf16[64,32,128]{2,1,0:T(8,128)(2,1)S(1)} %merge_rows.1), channel_id=1, replica_groups=mesh['grp'=8,'sub'=64] {'sub'}, dimensions={0} | all-to-all | bytes 1048576 | tf_op jit(solution)/shard_map/all_to_all | solution.py:342
  80.4 0.0 copy-done.1
  80.4 1.8 %owned_and_top.1 = (bf16[12,192,192]{2,1,0:T(8,128)(2,1)}, bf16[384,128]{1,0:T(8,128)(2,1)S(1)}) custom-call(bf16[64,32,128]{2,1,0:T(8,128)(2,1)S(1)} %all_to_all.25.z_ref, bf16[12,192,128]{2,1,0:T(8,128)(2,1)S(1)} %copy-done.1, bf16[256,128]{1,0:T(8,128)(2,1)S(1)} %fusion.rows_ref), custom_call_target="tpu_custom_call" | custom-call | tf_op jit(solution)/shard_map/owned_and_top/pallas_call | solution.py:303
  82.2 10.4 %all_to_all.26 = bf16[16,24,128]{2,1,0:T(8,128)(2,1)S(1)} all-to-all(bf16[16,24,128]{2,1,0:T(8,128)(2,1)S(1)} %bitcast.8), channel_id=1, replica_groups={{0,1,2,3,4,5,6,7,8,9,10,11,12,13,14,15},{16,17,18,19,20,21,22,23,24,25,..., dimensions={0} | all-to-all | bytes 196608 | tf_op jit(solution)/shard_map/all_to_all | solution.py:342
  92.6 19.1 %all_to_all.27 = bf16[32,24,128]{2,1,0:T(8,128)(2,1)S(1)} all-to-all(bf16[32,24,128]{2,1,0:T(8,128)(2,1)S(1)} %broadcast_in_dim.8), channel_id=1, replica_groups={{0,16,32,48,64,80,96,112,128,144,160,176,192,208,224,240,256,272,288,30..., dimensions={0} | all-to-all | bytes 393216 | tf_op jit(solution)/shard_map/all_to_all | solution.py:342
  111.8 11.5 %all_to_all.28 = f32[16,24,128]{2,1,0:T(8,128)S(1)} all-to-all(f32[16,24,128]{2,1,0:T(8,128)S(1)} %broadcast_in_dim.9), channel_id=1, replica_groups={{0,1,2,3,4,5,6,7,8,9,10,11,12,13,14,15},{16,17,18,19,20,21,22,23,24,25,..., dimensions={0} | all-to-all | bytes 393216 | tf_op jit(solution)/shard_map/all_to_all | solution.py:342
  123.3 0.8 mirror.1
  (4 shorter events, 0.1 us)
Async XLA Ops:
  0.6 20.3 %copy-start = (bf16[768,256]{1,0:T(8,128)(2,1)S(1)}, bf16[768,256]{1,0:T(8,128)(2,1)}, u32[]{:S(2)}) copy-start(bf16[768,256]{1,0:T(8,128)(2,1)} %param.17) | copy-start | bytes 1179652
  6.1 14.9 %copy-start.2 = (s32[128]{0:T(128)S(1)}, s32[128]{0:T(128)}, u32[]{:S(2)}) copy-start(s32[128]{0:T(128)} %param.16) | copy-start | bytes 1540
  6.1 48.5 %all-to-all-start = ((bf16[64,80,128]{2,1,0:T(8,128)(2,1)}), bf16[64,80,128]{2,1,0:T(8,128)(2,1)S(1)}, u32[]{:S(2)}, u32[]{:S(2)}) async-start(bf16[64,80,128]{2,1,0:T(8,128)(2,1)} %pack_faces.1), calls=%async_computation | async-start | bytes 2621440 | tf_op jit(solution)/shard_map/all_to_all | solution.py:342
  54.5 25.8 %copy-start.1 = (bf16[12,192,128]{2,1,0:T(8,128)(2,1)S(1)}, bf16[12,192,128]{2,1,0:T(8,128)(2,1)}, u32[]{:S(2)}) copy-start(bf16[12,192,128]{2,1,0:T(8,128)(2,1)} %basis_ref.1) | copy-start | bytes 1769476

commit v10 on v6

--- a/solution.py
+++ b/solution.py
@@ -69,10 +69,16 @@
     eye_right = eye & ~left
     for copy in copies[:2] + copies[-3:]:
         copy.wait()
-    for s in range(steps):
-        copies[2 + s].wait()
+    @pl.loop(0, steps)
+    def _(s):
+        part = pl.ds(s * STEP_FACES, STEP_FACES)
+        pltpu.make_async_copy(
+            coupling_hbm.at[part], coupling_ref.at[part], sems.at[2 + s]
+        ).wait()
+        diags = diag_ref[pl.ds(pl.multiple_of(s * STEP_FACES, STEP_FACES), STEP_FACES), :]
         interiors = []
-        for face in range(s * STEP_FACES, (s + 1) * STEP_FACES):
+        for q in range(STEP_FACES):
+            face = s * STEP_FACES + q
             c = coupling_ref[face]
             mid = c[:, Q : 2 * Q]
             columns = jnp.concatenate([c[:, 2 * Q :], mid, mid, c[:, :Q]], axis=1)
@@ -90,8 +96,8 @@
             face = s * STEP_FACES + q
             d3, r1 = g[:Q, :LANES], g[Q : 2 * Q, :LANES]
             t0, d1 = g[3 * Q :, :LANES], g[3 * Q :, LANES:]
-            diag01 = diag_ref[face : face + 1, :LANES]
-            diag2 = jnp.concatenate([diag_ref[face : face + 1, LANES:]] * 2, axis=1)
+            diag01 = diags[q : q + 1, :LANES]
+            diag2 = jnp.concatenate([diags[q : q + 1, LANES:]] * 2, axis=1)
             diag10 = swap_halves(diag01)
             t1 = jnp.where(eye_right, diag10, 0.0) - jnp.where(
                 left | ~keep, r1, d1
@@ -110,9 +116,9 @@
             f = jnp.where(keep, jnp.where(eye, diag2, 0.0) - d3, spare)
 
             def put(k, value):
-                scratch[pl.ds(k * Q * (pairs + 1) + face // 2, Q, stride=pairs + 1), :] = value
-
-            odd = face % 2
+                scratch[pl.ds(k * Q * (pairs + 1) + s * (STEP_FACES // 2) + q // 2, Q, stride=pairs + 1), :] = value
+
+            odd = q % 2
             put(2 * odd, -t0)
             put(2 * odd + 1, t1)
             if odd:

time: 125 us -> 125 us (level)
  no operation moved by 1% of the time
where the time goes in v10:
time: 125 us; the launch traced here: 124 us
  blocking collectives  64.8 us (52%)
  waiting for transfers between devices  33.2 us (27%)
  starting transfers between devices  14.8 us (12%)
  Pallas kernels  10.2 us (8%)
    all_to_all x4, blocking collectives, exchange(): lax.all_to_all(x, axis, split_axis=0, concat_axis=0, tiled=True, axis_ind...  64.8 us
    all_to_all x1, waiting for transfers between devices, exchange(): lax.all_to_all(x, axis, split_axis=0, concat_axis=0, tiled=True, axis_ind...  33.2 us
    all_to_all x1, starting transfers between devices, exchange(): lax.all_to_all(x, axis, split_axis=0, concat_axis=0, tiled=True, axis_ind...  14.8 us
    pallas_call x1, Pallas kernels, pack_faces(): pl.pallas_call(schur_kernel, in_specs=[pl.BlockSpec(memory_space=pl.ANY)]...  5.64 us
  transfers between devices with their start and end apart: 1, of which 1 were waited for; matrix products, arithmetic and copies ran while one was open for 0% of the time, Pallas kernels for 0%

profile of v10, /device:TPU:1, one launch (start us, length us, event | category | flops | bytes accessed | tf_op | source)
XLA Modules:
  0.0 124.3 jit_solution(10159841713506023680)
XLA Ops:
  0.6 0.0 copy-start
  0.6 5.6 %pack_faces.1 = bf16[64,80,128]{2,1,0:T(8,128)(2,1)} custom-call(s32[32]{0:T(128)} %block_hbm.1, s32[32]{0:T(128)} %bitcast.9, s32[32]{0:T(128)} %slot_hbm.1, bf16[32,192,192]{2,1,0:T(8,128)(2,1)} %coupling_hbm.1, bf16[4,192,192]{2,1,0:T(8,128)(2,1)} %factors_hbm.1, f32[32,192]{1,0:T(8,128)} %diag_hbm.1), custom_call_target="tpu_custom_call" | custom-call | tf_op jit(solution)/shard_map/pack_faces/pallas_call | solution.py:136
  6.3 0.0 copy-start.2
  6.3 14.8 %all-to-all-start = ((bf16[64,80,128]{2,1,0:T(8,128)(2,1)}), bf16[64,80,128]{2,1,0:T(8,128)(2,1)S(1)}, u32[]{:S(2)}, u32[]{:S(2)}) async-start(bf16[64,80,128]{2,1,0:T(8,128)(2,1)} %pack_faces.1), calls=%async_computation | async-start | bytes 2621440 | tf_op jit(solution)/shard_map/all_to_all | solution.py:348
  21.2 0.0 copy-done
  21.2 0.0 copy-done.2
  21.2 0.4 fusion.rows_ref
  21.5 33.2 %all-to-all-done.x_ref = bf16[64,80,128]{2,1,0:T(8,128)(2,1)S(1)} async-done(((bf16[64,80,128]{2,1,0:T(8,128)(2,1)}), bf16[64,80,128]{2,1,0:T(8,128)(2,1)S(1)}, u32[]{:S(2)}, u32[]{:S(2)}) %all-to-all-start) | async-done | bytes 1310752 | tf_op jit(solution)/shard_map/all_to_all | solution.py:348
  54.8 0.0 copy-start.1
  54.8 2.0 %merge_rows.1 = bf16[64,32,128]{2,1,0:T(8,128)(2,1)S(1)} custom-call(s32[1]{0:T(128)} %bitcast.me_ref, bf16[64,80,128]{2,1,0:T(8,128)(2,1)S(1)} %all-to-all-done.x_ref), custom_call_target="tpu_custom_call" | custom-call | tf_op jit(solution)/shard_map/merge_rows/pallas_call | solution.py:221
  56.7 23.8 %all_to_all.25.z_ref = bf16[64,32,128]{2,1,0:T(8,128)(2,1)S(1)} all-to-all(bf16[64,32,128]{2,1,0:T(8,128)(2,1)S(1)} %merge_rows.1), channel_id=1, replica_groups=mesh['grp'=8,'sub'=64] {'sub'}, dimensions={0} | all-to-all | bytes 1048576 | tf_op jit(solution)/shard_map/all_to_all | solution.py:348
  80.6 0.0 copy-done.1
  80.6 1.8 %owned_and_top.1 = (bf16[12,192,192]{2,1,0:T(8,128)(2,1)}, f32[384,128]{1,0:T(8,128)S(1)}) custom-call(bf16[64,32,128]{2,1,0:T(8,128)(2,1)S(1)} %all_to_all.25.z_ref, bf16[12,192,128]{2,1,0:T(8,128)(2,1)S(1)} %copy-done.1, bf16[256,128]{1,0:T(8,128)(2,1)S(1)} %fusion.rows_ref), custom_call_target="tpu_custom_call" | custom-call | tf_op jit(solution)/shard_map/owned_and_top/pallas_call | solution.py:309
  82.4 10.4 %all_to_all.26 = bf16[16,24,128]{2,1,0:T(8,128)(2,1)S(1)} all-to-all(bf16[16,24,128]{2,1,0:T(8,128)(2,1)S(1)} %bitcast.8), channel_id=1, replica_groups={{0,1,2,3,4,5,6,7,8,9,10,11,12,13,14,15},{16,17,18,19,20,21,22,23,24,25,..., dimensions={0} | all-to-all | bytes 196608 | tf_op jit(solution)/shard_map/all_to_all | solution.py:348
  92.9 19.1 %all_to_all.27 = bf16[32,24,128]{2,1,0:T(8,128)(2,1)S(1)} all-to-all(bf16[32,24,128]{2,1,0:T(8,128)(2,1)S(1)} %broadcast_in_dim.8), channel_id=1, replica_groups={{0,16,32,48,64,80,96,112,128,144,160,176,192,208,224,240,256,272,288,30..., dimensions={0} | all-to-all | bytes 393216 | tf_op jit(solution)/shard_map/all_to_all | solution.py:348
  112.0 11.5 %all_to_all.28 = f32[16,24,128]{2,1,0:T(8,128)S(1)} all-to-all(f32[16,24,128]{2,1,0:T(8,128)S(1)} %broadcast_in_dim.9), channel_id=1, replica_groups={{0,1,2,3,4,5,6,7,8,9,10,11,12,13,14,15},{16,17,18,19,20,21,22,23,24,25,..., dimensions={0} | all-to-all | bytes 393216 | tf_op jit(solution)/shard_map/all_to_all | solution.py:348
  123.5 0.8 mirror.1
  (5 shorter events, 0.1 us)
Async XLA Ops:
  0.6 20.5 %copy-start = (bf16[768,256]{1,0:T(8,128)(2,1)S(1)}, bf16[768,256]{1,0:T(8,128)(2,1)}, u32[]{:S(2)}) copy-start(bf16[768,256]{1,0:T(8,128)(2,1)} %param.17) | copy-start | bytes 1179652
  6.3 14.9 %copy-start.2 = (s32[128]{0:T(128)S(1)}, s32[128]{0:T(128)}, u32[]{:S(2)}) copy-start(s32[128]{0:T(128)} %param.16) | copy-start | bytes 1540
  6.3 48.5 %all-to-all-start = ((bf16[64,80,128]{2,1,0:T(8,128)(2,1)}), bf16[64,80,128]{2,1,0:T(8,128)(2,1)S(1)}, u32[]{:S(2)}, u32[]{:S(2)}) async-start(bf16[64,80,128]{2,1,0:T(8,128)(2,1)} %pack_faces.1), calls=%async_computation | async-start | bytes 2621440 | tf_op jit(solution)/shard_map/all_to_all | solution.py:348
  54.8 25.8 %copy-start.1 = (bf16[12,192,128]{2,1,0:T(8,128)(2,1)S(1)}, bf16[12,192,128]{2,1,0:T(8,128)(2,1)}, u32[]{:S(2)}) copy-start(bf16[12,192,128]{2,1,0:T(8,128)(2,1)} %basis_ref.1) | copy-start | bytes 1769476
